TPU v7x, 32 devices: a whole 2x2x4 slice. The times are simulated.
32 devices in a mesh: rep: 4 (over z), seq: 4 (over y, core), shard: 2 (over x).
Axes of the slice: x: 2, y: 2, z: 4, core: 2. Of those that a mesh axis runs over, the one named last changes fastest.
Arguments:
- tokens: bfloat16 [8, 1024, 1024], P(('rep', 'shard'), 'seq'), may hold values from -6 to 6
- cotangent: bfloat16 [8, 1024, 1024], P(('rep', 'shard'), 'seq'), may hold values from -6 to 6
- in_proj: bfloat16 [1024, 3072], P('shard'), may hold values from -0.1875 to 0.1875
- in_moment: bfloat16 [1024, 3072], P('shard'), may hold values from -64 to 64
- in_square: bfloat16 [1024, 3072], P('shard'), may hold values from 434 to 1720
- out_proj: bfloat16 [1024, 1024], P('shard'), may hold values from -0.1875 to 0.1875
- out_moment: bfloat16 [1024, 1024], P('shard'), may hold values from -80 to 80
- out_square: bfloat16 [1024, 1024], P('shard'), may hold values from 860 to 3440
- gate_up: bfloat16 [2, 1024, 4608], P(None, 'shard'), may hold values from -0.1875 to 0.1875
- gate_moment: bfloat16 [2, 1024, 4608], P(None, 'shard'), may hold values from -20 to 20
- gate_square: bfloat16 [2, 1024, 4608], P(None, 'shard'), may hold values from 43.25 to 172
- down_proj: bfloat16 [4608, 1024], P(None, 'shard'), may hold values from -0.09375 to 0.09375
- down_moment: bfloat16 [4608, 1024], P(None, 'shard'), may hold values from -40 to 40
- down_square: bfloat16 [4608, 1024], P(None, 'shard'), may hold values from 172 to 688
- conv_kernel: bfloat16 [3, 1024], P(None, 'shard'), may hold values from -3.5 to 3.5
- conv_moment: bfloat16 [3, 1024], P(None, 'shard'), may hold values from -80 to 80
- conv_square: bfloat16 [3, 1024], P(None, 'shard'), may hold values from 860 to 3440
- norm_gains: bfloat16 [2, 1024], P(None, 'shard'), may hold values from 0.5 to 1.5
- gains_moment: bfloat16 [2, 1024], P(None, 'shard'), may hold values from -80 to 80
- gains_square: bfloat16 [2, 1024], P(None, 'shard'), may hold values from 860 to 3440
Outputs:
- block_out: bfloat16 [8, 1024, 1024], P(('rep', 'shard'), 'seq')
- token_grad: bfloat16 [8, 1024, 1024], P(('rep', 'shard'), 'seq')
- in_next: float32 [1024, 3072], P('shard')
- in_moment_next: float32 [1024, 3072], P('shard')
- in_square_next: float32 [1024, 3072], P('shard')
- out_next: float32 [1024, 1024], P('shard')
- out_moment_next: float32 [1024, 1024], P('shard')
- out_square_next: float32 [1024, 1024], P('shard')
- gate_next: float32 [2, 1024, 4608], P(None, 'shard')
- gate_moment_next: float32 [2, 1024, 4608], P(None, 'shard')
- gate_square_next: float32 [2, 1024, 4608], P(None, 'shard')
- down_next: float32 [4608, 1024], P(None, 'shard')
- down_moment_next: float32 [4608, 1024], P(None, 'shard')
- down_square_next: float32 [4608, 1024], P(None, 'shard')
- conv_next: float32 [3, 1024], P(None, 'shard')
- conv_moment_next: float32 [3, 1024], P(None, 'shard')
- conv_square_next: float32 [3, 1024], P(None, 'shard')
- gains_next: float32 [2, 1024], P(None, 'shard')
- gains_moment_next: float32 [2, 1024], P(None, 'shard')
- gains_square_next: float32 [2, 1024], P(None, 'shard')
All inputs are finite; a program needn't handle non-finite values.
Results may differ from a plain program's by a relative error of at most 0.008.
Values may be sent and summed in bfloat16 or wider, within the bound.
A program may use at most 512 MiB of HBM per device.

v0:
```python
import jax
import jax.numpy as jnp
from jax import lax
from jax.sharding import PartitionSpec as P

D = 1024
FF = 4608
STEP = 10


norm_eps = 1e-05
beta_one = 0.9
beta_two = 0.95
adam_eps = 1e-08
decay_rate = 0.1
small_rate = 0.4


def shifted(block, axis, distance):
    devices = range(lax.axis_size(axis))
    route = [(i - distance, i) for i in devices if i - distance in devices]
    return lax.ppermute(block, axis, route)


def norm_forward(values, gain_vector):
    norm_scale = lax.rsqrt(jnp.mean(values * values, axis=-1, keepdims=True) + norm_eps)
    unit_rows = values * norm_scale
    return (unit_rows, norm_scale, (unit_rows * gain_vector).astype(jnp.bfloat16))


def norm_backward(grad_normed, unit_rows, norm_scale, gain_vector):
    gain_grad = jnp.sum(grad_normed * unit_rows, axis=(0, 1))
    grad_unit = grad_normed * gain_vector
    grad_values = norm_scale * (
        grad_unit - unit_rows * jnp.mean(grad_unit * unit_rows, axis=-1, keepdims=True)
    )
    return (gain_grad, grad_values)


def adamw(weight, first_moment, second_moment, gradient, step_rate, decay_factor):
    first_new = beta_one * first_moment + (1.0 - beta_one) * gradient
    second_new = beta_two * second_moment + (1.0 - beta_two) * gradient * gradient
    adam_ratio = (
        first_new
        / (1.0 - beta_one**STEP)
        / (jnp.sqrt(second_new / (1.0 - beta_two**STEP)) + adam_eps)
    )
    weight_new = weight - step_rate * (adam_ratio + decay_factor * weight)
    return (weight_new, first_new, second_new)


def body(
    tokens,
    cotangent,
    in_proj,
    in_moment,
    in_square,
    out_proj,
    out_moment,
    out_square,
    gate_up,
    gate_moment,
    gate_square,
    down_proj,
    down_moment,
    down_square,
    conv_kernel,
    conv_moment,
    conv_square,
    norm_gains,
    gains_moment,
    gains_square,
):
    gathered = (
        lax.all_gather(in_proj, "shard", axis=0, tiled=True),
        lax.all_gather(out_proj, "shard", axis=0, tiled=True),
        lax.all_gather(gate_up, "shard", axis=1, tiled=True),
        lax.all_gather(down_proj, "shard", axis=1, tiled=True),
        lax.all_gather(conv_kernel, "shard", axis=1, tiled=True),
        lax.all_gather(norm_gains, "shard", axis=1, tiled=True),
    )
    full_in, full_out, full_gate, full_down, full_conv, full_gains = gathered
    gains_float = full_gains.astype(jnp.float32)
    conv_float = full_conv.astype(jnp.float32)
    inputs = tokens.astype(jnp.float32)
    model_width = inputs.shape[2]
    rows_count = inputs.shape[1]
    unit_one, scale_one, normed_one = norm_forward(inputs, gains_float[0])
    projected = jnp.einsum("scd,de->sce", normed_one, full_in, preferred_element_type=jnp.float32)
    first_gate = projected[:, :, :model_width]
    second_gate = projected[:, :, model_width : 2 * model_width]
    conv_input = projected[:, :, 2 * model_width :]
    mixed_in = (first_gate * conv_input).astype(jnp.bfloat16)
    before = shifted(mixed_in[:, rows_count - 2 :, :], "seq", 1)
    extended = jnp.concatenate([before, mixed_in], axis=1).astype(jnp.float32)
    convolved = (
        conv_float[0] * extended[:, :-2]
        + conv_float[1] * extended[:, 1:-1]
        + conv_float[2] * extended[:, 2:]
    )
    gated_out = (second_gate * convolved).astype(jnp.bfloat16)
    middle = inputs + jnp.einsum(
        "scd,de->sce", gated_out, full_out, preferred_element_type=jnp.float32
    )
    unit_two, scale_two, normed_two = norm_forward(middle, gains_float[1])
    gate_value = jnp.einsum(
        "scd,df->scf", normed_two, full_gate[0], preferred_element_type=jnp.float32
    )
    upward = jnp.einsum("scd,df->scf", normed_two, full_gate[1], preferred_element_type=jnp.float32)
    hidden = (jax.nn.silu(gate_value) * upward).astype(jnp.bfloat16)
    result = middle + jnp.einsum(
        "scf,fd->scd", hidden, full_down, preferred_element_type=jnp.float32
    )
    block_out = result.astype(jnp.bfloat16)
    regathered = (
        lax.all_gather(in_proj, "shard", axis=0, tiled=True),
        lax.all_gather(out_proj, "shard", axis=0, tiled=True),
        lax.all_gather(gate_up, "shard", axis=1, tiled=True),
        lax.all_gather(down_proj, "shard", axis=1, tiled=True),
        lax.all_gather(conv_kernel, "shard", axis=1, tiled=True),
        lax.all_gather(norm_gains, "shard", axis=1, tiled=True),
    )
    full_in, full_out, full_gate, full_down, full_conv, full_gains = regathered
    gains_float = full_gains.astype(jnp.float32)
    conv_float = full_conv.astype(jnp.float32)
    grad_result = cotangent.astype(jnp.float32)
    grad_hidden = jnp.einsum(
        "scd,fd->scf", cotangent, full_down, preferred_element_type=jnp.float32
    )
    grad_down = jnp.einsum("scf,scd->fd", hidden, cotangent, preferred_element_type=jnp.float32)
    sigmoid_gate = jax.nn.sigmoid(gate_value)
    grad_gate = (
        grad_hidden * upward * sigmoid_gate * (1.0 + gate_value * (1.0 - sigmoid_gate))
    ).astype(jnp.bfloat16)
    grad_upward = (grad_hidden * jax.nn.silu(gate_value)).astype(jnp.bfloat16)
    grad_gate_up = jnp.stack(
        [
            jnp.einsum("scd,scf->df", normed_two, grad_gate, preferred_element_type=jnp.float32),
            jnp.einsum("scd,scf->df", normed_two, grad_upward, preferred_element_type=jnp.float32),
        ]
    )
    grad_normed_two = jnp.einsum(
        "scf,df->scd", grad_gate, full_gate[0], preferred_element_type=jnp.float32
    ) + jnp.einsum("scf,df->scd", grad_upward, full_gate[1], preferred_element_type=jnp.float32)
    gain_two, grad_from_two = norm_backward(grad_normed_two, unit_two, scale_two, gains_float[1])
    grad_middle = grad_result + grad_from_two
    middle_low = grad_middle.astype(jnp.bfloat16)
    grad_out = jnp.einsum("scd,sce->de", gated_out, middle_low, preferred_element_type=jnp.float32)
    grad_gated = jnp.einsum("sce,de->scd", middle_low, full_out, preferred_element_type=jnp.float32)
    grad_second = grad_gated * convolved
    grad_conv_out = grad_gated * second_gate
    grad_conv = jnp.stack(
        [
            jnp.sum(grad_conv_out * extended[:, offset : offset + rows_count], axis=(0, 1))
            for offset in range(3)
        ]
    )
    grad_extended = (
        jnp.pad(grad_conv_out * conv_float[0], ((0, 0), (0, 2), (0, 0)))
        + jnp.pad(grad_conv_out * conv_float[1], ((0, 0), (1, 1), (0, 0)))
        + jnp.pad(grad_conv_out * conv_float[2], ((0, 0), (2, 0), (0, 0)))
    )
    from_next = shifted(grad_extended[:, :2, :], "seq", -1)
    grad_mixed = grad_extended[:, 2:, :] + jnp.pad(from_next, ((0, 0), (rows_count - 2, 0), (0, 0)))
    grad_projected = jnp.concatenate(
        [grad_mixed * conv_input, grad_second, grad_mixed * first_gate], axis=2
    ).astype(jnp.bfloat16)
    grad_in = jnp.einsum(
        "scd,sce->de", normed_one, grad_projected, preferred_element_type=jnp.float32
    )
    grad_normed_one = jnp.einsum(
        "sce,de->scd", grad_projected, full_in, preferred_element_type=jnp.float32
    )
    gain_one, grad_from_one = norm_backward(grad_normed_one, unit_one, scale_one, gains_float[0])
    token_grad = (grad_middle + grad_from_one).astype(jnp.bfloat16)
    grad_gains = jnp.stack([gain_one, gain_two])
    parts = (
        lax.psum_scatter(grad_in, "shard", scatter_dimension=0, tiled=True),
        lax.psum_scatter(grad_out, "shard", scatter_dimension=0, tiled=True),
        lax.psum_scatter(grad_gate_up, "shard", scatter_dimension=1, tiled=True),
        lax.psum_scatter(grad_down, "shard", scatter_dimension=1, tiled=True),
        lax.psum_scatter(grad_conv, "shard", scatter_dimension=1, tiled=True),
        lax.psum_scatter(grad_gains, "shard", scatter_dimension=1, tiled=True),
    )
    totals = lax.psum((parts[0], parts[1], parts[2], parts[3], parts[4], parts[5]), ("rep", "seq"))
    matrix_rate = 2.0 * D ** (-0.5)
    down_rate = 2.0 * FF ** (-0.5)
    in_next, in_moment_next, in_square_next = adamw(
        in_proj.astype(jnp.float32),
        in_moment.astype(jnp.float32),
        in_square.astype(jnp.float32),
        totals[0],
        matrix_rate,
        decay_rate,
    )
    out_next, out_moment_next, out_square_next = adamw(
        out_proj.astype(jnp.float32),
        out_moment.astype(jnp.float32),
        out_square.astype(jnp.float32),
        totals[1],
        matrix_rate,
        decay_rate,
    )
    gate_next, gate_moment_next, gate_square_next = adamw(
        gate_up.astype(jnp.float32),
        gate_moment.astype(jnp.float32),
        gate_square.astype(jnp.float32),
        totals[2],
        matrix_rate,
        decay_rate,
    )
    down_next, down_moment_next, down_square_next = adamw(
        down_proj.astype(jnp.float32),
        down_moment.astype(jnp.float32),
        down_square.astype(jnp.float32),
        totals[3],
        down_rate,
        decay_rate,
    )
    conv_next, conv_moment_next, conv_square_next = adamw(
        conv_kernel.astype(jnp.float32),
        conv_moment.astype(jnp.float32),
        conv_square.astype(jnp.float32),
        totals[4],
        small_rate,
        0.0,
    )
    gains_next, gains_moment_next, gains_square_next = adamw(
        norm_gains.astype(jnp.float32),
        gains_moment.astype(jnp.float32),
        gains_square.astype(jnp.float32),
        totals[5],
        small_rate,
        0.0,
    )
    return (
        block_out,
        token_grad,
        in_next,
        in_moment_next,
        in_square_next,
        out_next,
        out_moment_next,
        out_square_next,
        gate_next,
        gate_moment_next,
        gate_square_next,
        down_next,
        down_moment_next,
        down_square_next,
        conv_next,
        conv_moment_next,
        conv_square_next,
        gains_next,
        gains_moment_next,
        gains_square_next,
    )


def solution(mesh):
    in_specs = (
        P(("rep", "shard"), "seq", None),
        P(("rep", "shard"), "seq", None),
        P("shard", None),
        P("shard", None),
        P("shard", None),
        P("shard", None),
        P("shard", None),
        P("shard", None),
        P(None, "shard", None),
        P(None, "shard", None),
        P(None, "shard", None),
        P(None, "shard"),
        P(None, "shard"),
        P(None, "shard"),
        P(None, "shard"),
        P(None, "shard"),
        P(None, "shard"),
        P(None, "shard"),
        P(None, "shard"),
        P(None, "shard"),
    )
    out_specs = (
        P(("rep", "shard"), "seq", None),
        P(("rep", "shard"), "seq", None),
        P("shard", None),
        P("shard", None),
        P("shard", None),
        P("shard", None),
        P("shard", None),
        P("shard", None),
        P(None, "shard", None),
        P(None, "shard", None),
        P(None, "shard", None),
        P(None, "shard"),
        P(None, "shard"),
        P(None, "shard"),
        P(None, "shard"),
        P(None, "shard"),
        P(None, "shard"),
        P(None, "shard"),
        P(None, "shard"),
        P(None, "shard"),
    )
    return jax.shard_map(body, mesh=mesh, in_specs=in_specs, out_specs=out_specs, check_vma=False)
```

profile of v0, /device:TPU:0, one launch (start us, length us, event | category | flops | bytes accessed | tf_op | source)
XLA Modules:
  0.0 2072.9 jit_solution(15756460145349208346)
XLA Ops:
  10.1 5.2 all_gather.24
  15.3 4.3 all_gather.26
  19.8 72.8 %all-gather.5.cloned.1.call-done = bf16[1024,3072]{1,0:T(8,128)(2,1)} async-done(((bf16[512,3072]{1,0:T(8,128)(2,1)}), bf16[1024,3072]{1,0:T(8,128)(2,1)}) %all-gather.5.cloned.1.call-update) | async-done | bytes 6291472 | tf_op jit(solution)/shard_map/all_gather | solution.py:75
  92.7 4.7 convolution_bitcast_fusion.2
  97.5 1.7 collective-permute-start
  99.3 0.8 collective-permute-done
  100.2 1.3 fusion.38
  101.6 25.8 %all-gather.7.cloned.1.call-done = bf16[1024,1024]{1,0:T(8,128)(2,1)} async-done(((bf16[512,1024]{1,0:T(8,128)(2,1)}), bf16[1024,1024]{1,0:T(8,128)(2,1)}) %all-gather.7.cloned.1.call-update) | async-done | bytes 2097168 | tf_op jit(solution)/shard_map/all_gather | solution.py:76
  127.4 2.4 multiply_reduce_fusion.3
  130.0 224.0 %all-gather.9.cloned.1.call-done = bf16[2,1024,4608]{2,1,0:T(8,128)(2,1)} async-done(((bf16[2,512,4608]{2,1,0:T(8,128)(2,1)}), bf16[2,1024,4608]{2,1,0:T(8,128)(2,1)}) %all-gather.9.cloned.1.call-update) | async-done | bytes 18874384 | tf_op jit(solution)/shard_map/all_gather | solution.py:77
  354.0 8.9 fusion.7
  362.9 2.7 copy-done.28
  365.6 4.2 fusion.9
  369.8 103.6 %all-gather.11.cloned.1.call-done = bf16[4608,1024]{1,0:T(8,128)(2,1)} async-done(((bf16[4608,512]{1,0:T(8,128)(2,1)}), bf16[4608,1024]{1,0:T(8,128)(2,1)}) %all-gather.11.cloned.1.call-update) | async-done | bytes 9437200 | tf_op jit(solution)/shard_map/all_gather | solution.py:78
  473.5 9.9 multiply_convert_fusion
  483.4 6.9 fusion.6
  490.3 5.6 fusion.32
  496.2 2.8 fusion.44
  499.3 2.3 convolution_bitcast_fusion.3
  501.7 2.1 multiply_reduce_fusion.2
  504.2 1.6 collective-permute-start.1
  506.2 1.3 collective-permute-done.1
  508.7 6.7 fusion.36
  515.5 1.0 copy-done.15
  516.5 9.9 fusion.47
  526.5 1.0 copy-done.5
  527.5 4.5 convolution_bitcast_fusion
  531.9 8.3 convolution_bitcast_fusion.1
  540.2 20.9 %pad_maximum_fusion = f32[2,1024,4608]{2,1,0:T(8,128)} fusion(f32[1,1024,4608]{2,1,0:T(8,128)S(1)} %convolution_bitcast_fusion, f32[1,1024,4608]{2,1,0:T(8,128)} %convolution_bitcast_fusion.1), kind=kLoop, calls=%fused_computation | loop fusion | flops 9437184 | bytes 75497472 | tf_op jit(solution)/shard_map/stack | solution.py:136
  561.3 1.0 copy.40
  562.4 6.4 fusion.30
  568.8 1.0 copy.42
  569.9 10.3 all-reduce.8.cloned.1.call-start
  580.2 120.6 %reduce-scatter.11.cloned.1.call-done = f32[512,3072]{1,0:T(8,128)} async-done(((f32[1024,3072]{1,0:T(8,128)}), f32[512,3072]{1,0:T(8,128)}) %reduce-scatter.11.cloned.1.call-update) | async-done | bytes 6291472 | tf_op jit(solution)/shard_map/reduce_scatter | solution.py:178
  700.8 214.7 %reduce-scatter.17.cloned.1.call-done = f32[4608,512]{1,0:T(8,128)} async-done(((f32[4608,1024]{1,0:T(8,128)}), f32[4608,512]{1,0:T(8,128)}) %reduce-scatter.17.cloned.1.call-update) | async-done | bytes 9437200 | tf_op jit(solution)/shard_map/reduce_scatter | solution.py:181
  915.5 416.4 %reduce-scatter.15.cloned.1.call-done = f32[2,512,4608]{2,1,0:T(8,128)} async-done(((f32[2,1024,4608]{2,1,0:T(8,128)}), f32[2,512,4608]{2,1,0:T(8,128)}) %reduce-scatter.15.cloned.1.call-update) | async-done | bytes 18874384 | tf_op jit(solution)/shard_map/reduce_scatter | solution.py:180
  1331.9 7.9 fusion.23
  1339.8 1.1 fusion.29
  1340.9 8.4 reduce-scatter.19.cloned.1.call-done
  1349.4 1.1 copy.41
  1350.4 16.2 reduce-scatter.21.cloned.1.call-done
  1366.6 1.1 copy.43
  1367.7 64.4 %all-reduce.4 = (f32[3,512]{1,0:T(4,128)S(1)}, f32[2,512]{1,0:T(2,128)S(1)}) all-reduce(f32[3,512]{1,0:T(4,128)S(1)} %copy.41, f32[2,512]{1,0:T(2,128)S(1)} %copy.43), channel_id=1, replica_groups=mesh['rep'=4,'seq'=4,'shard'=2] {'rep','seq'}, use_global_device_ids=true, to_apply=%region_16.17 | all-reduce | flops 2560 | bytes 20480 | tf_op jit(solution)/shard_map/psum | solution.py:185
  1433.4 560.2 %all-reduce.8.cloned.1.call-done = (f32[512,3072]{1,0:T(8,128)}, f32[512,1024]{1,0:T(8,128)}, f32[2,512,4608]{2,1,0:T(8,128)}, f32[4608,512]{1,0:T(8,128)}) async-done(((f32[512,3072]{1,0:T(8,128)}, f32[512,1024]{1,0:T(8,128)}, f32[2,512,4608]{2,1,0:T(8,128)}, f32[4608,512]{1,0:T(8,128)}), (f32[512,3072]{1,0:T(8,128)}, f32[512,1024]{1,0:T(8,128)}, f32[2,512,4608]{2,1,0:T(8,128)}, ...) | async-done | bytes 36700176 | tf_op jit(solution)/shard_map/psum | solution.py:185
  1993.6 14.1 convert_subtract_fusion.2
  2007.7 4.1 convert_subtract_fusion.3
  2011.8 35.9 %convert_subtract_fusion = (f32[2,512,4608]{2,1,0:T(8,128)}, f32[2,512,4608]{2,1,0:T(8,128)}, f32[2,512,4608]{2,1,0:T(8,128)}) fusion(bf16[2,512,4608]{2,1,0:T(8,128)(2,1)S(1)} %bitcast.107, f32[2,512,4608]{2,1,0:T(8,128)} %get-tuple-element.31, bf16[2,512,4608]{2,1,0:T(8,128)(2,1)} %param.29, bf16[2,512,4608]{2,1,0:T(8,128)(2,1)} %param.30), kind=kLoop, calls=%fused_computation.2 | loop fusion | flops 84934656 | bytes 103809024 | tf_op jit(solution)/shard_map/sub | solution.py:48
  2047.7 18.5 convert_subtract_fusion.1
  (109 shorter events, 7.8 us)
Async XLA Ops:
  7.2 85.5 %all-gather.5.cloned.1.call-start = ((), (), s32[]{:S(2)}) async-start(), calls=%async_computation.6 | async-start | bytes 9437184 | tf_op jit(solution)/shard_map/all_gather | solution.py:75
  7.9 119.4 %all-gather.7.cloned.1.call-start = ((), (), s32[]{:S(2)}) async-start(), calls=%async_computation.7 | async-start | bytes 3145728 | tf_op jit(solution)/shard_map/all_gather | solution.py:76
  8.7 1.4 copy-start.23
  8.7 6.6 copy-start.22
  8.7 10.9 copy-start.2
  8.7 345.3 %all-gather.9.cloned.1.call-start = ((), (), s32[]{:S(2)}) async-start(), calls=%async_computation.8 | async-start | bytes 28311552 | tf_op jit(solution)/shard_map/all_gather | solution.py:77
  9.4 464.0 %all-gather.11.cloned.1.call-start = ((), (), s32[]{:S(2)}) async-start(), calls=%async_computation.9 | async-start | bytes 14155776 | tf_op jit(solution)/shard_map/all_gather | solution.py:78
  10.0 570.2 %reduce-scatter.13.cloned.1.call-start = ((), (), s32[]{:S(2)}) async-start(), calls=%async_computation.11 | async-start | bytes 6291456 | tf_op jit(solution)/shard_map/reduce_scatter | solution.py:179
  97.3 2.9 copy-start
  97.5 2.6 collective-permute-start
  101.6 261.4 %copy-start.6 = (bf16[256,1024]{1,0:T(8,128)(2,1)}, bf16[256,1024]{1,0:T(8,128)(2,1)S(1)}, u32[]{:S(2)}) copy-start(bf16[256,1024]{1,0:T(8,128)(2,1)S(1)} %get-tuple-element.52) | copy-start | bytes 1572868
  129.9 233.0 %copy-start.4 = (bf16[256,1024]{1,0:T(8,128)(2,1)}, bf16[256,1024]{1,0:T(8,128)(2,1)S(1)}, u32[]{:S(2)}) copy-start(bf16[256,1024]{1,0:T(8,128)(2,1)S(1)} %fusion.39) | copy-start | bytes 1572868
  354.0 11.6 copy-start.28
  483.4 6.9 copy-start.9
  483.4 6.9 copy-start.11
  490.3 5.6 copy-start.14
  490.3 5.9 copy-start.7
  499.0 201.8 %reduce-scatter.11.cloned.1.call-start = ((), (), s32[]{:S(2)}) async-start(), calls=%async_computation.10 | async-start | bytes 18874368 | tf_op jit(solution)/shard_map/reduce_scatter | solution.py:178
  503.8 4.2 copy-start.12
  503.8 3.8 copy-start.1
  504.2 4.6 copy-start.3
  504.2 3.3 collective-permute-start.1
  507.9 0.8 copy-start.18
  507.9 7.5 copy-start.17
  515.4 1.0 copy-start.15
  515.5 400.0 %reduce-scatter.17.cloned.1.call-start = ((), (), s32[]{:S(2)}) async-start(), calls=%async_computation.13 | async-start | bytes 28311552 | tf_op jit(solution)/shard_map/reduce_scatter | solution.py:181
  526.4 1.0 copy-start.5
  526.4 805.4 %reduce-scatter.15.cloned.1.call-start = ((), (), s32[]{:S(2)}) async-start(), calls=%async_computation.12 | async-start | bytes 56623104 | tf_op jit(solution)/shard_map/reduce_scatter | solution.py:180
  527.5 4.5 copy-start.10
  561.2 1.2 copy-start.13
  561.2 788.1 %reduce-scatter.19.cloned.1.call-start = ((), (), s32[]{:S(2)}) async-start(), calls=%async_computation.14 | async-start | bytes 786432
  562.3 804.3 %reduce-scatter.21.cloned.1.call-start = ((), (), s32[]{:S(2)}) async-start(), calls=%async_computation.15 | async-start | bytes 786432
  569.9 1423.7 %all-reduce.8.cloned.1.call-start = ((), (), s32[]{:S(2)}) async-start(), calls=%async_computation.16 | async-start | bytes 73400320 | tf_op jit(solution)/shard_map/psum | solution.py:185
  1331.9 7.9 copy-start.19
  1331.9 100.2 %copy-start.26 = (bf16[2,512]{1,0:T(2,128)(2,1)S(1)}, bf16[2,512]{1,0:T(2,128)(2,1)}, u32[]{:S(2)}) copy-start(bf16[2,512]{1,0:T(2,128)(2,1)} %param.38) | copy-start | bytes 6148
  1331.9 100.2 %copy-start.27 = (bf16[2,512]{1,0:T(2,128)(2,1)S(1)}, bf16[2,512]{1,0:T(2,128)(2,1)}, u32[]{:S(2)}) copy-start(bf16[2,512]{1,0:T(2,128)(2,1)} %param.39) | copy-start | bytes 6148
  1331.9 100.8 %copy-start.24 = (bf16[3,512]{1,0:T(4,128)(2,1)S(1)}, bf16[3,512]{1,0:T(4,128)(2,1)}, u32[]{:S(2)}) copy-start(bf16[3,512]{1,0:T(4,128)(2,1)} %param.35) | copy-start | bytes 9220
  1331.9 100.8 %copy-start.25 = (bf16[3,512]{1,0:T(4,128)(2,1)S(1)}, bf16[3,512]{1,0:T(4,128)(2,1)}, u32[]{:S(2)}) copy-start(bf16[3,512]{1,0:T(4,128)(2,1)} %param.36) | copy-start | bytes 9220
  1993.6 18.2 slice-start
  1993.6 14.1 copy-start.8
  1993.6 14.1 copy-start.16
  1993.6 14.1 copy-start.20
  1993.6 14.1 copy-start.21
  1993.6 18.2 slice-start.1
  1993.6 18.2 slice-start.2
  2007.7 40.0 %slice-start.3 = ((s8[4718592]{0:T(1024)(128)(4,1)}), s8[4194304]{0:T(1024)(128)(4,1)S(1)}, s32[]{:S(2)}) async-start(s8[4718592]{0:T(1024)(128)(4,1)} %bitcast.108), calls=%async_computation.20 | async-start | bytes 8388608
  2011.8 35.9 %slice-start.4 = ((s8[4718592]{0:T(1024)(128)(4,1)}), s8[524288]{0:T(1024)(128)(4,1)S(1)}, s32[]{:S(2)}) async-start(s8[4718592]{0:T(1024)(128)(4,1)} %bitcast.108), calls=%async_computation.21 | async-start | bytes 1048576
Sparse Core Ops, SparseCore 0:
  9.6 83.0 all-gather.4
  94.2 33.1 all-gather.6
  128.9 225.0 all-gather.8
  355.4 117.9 all-gather.10
  499.1 54.2 reduce-scatter.12
  556.3 144.4 reduce-scatter.10
  703.8 211.6 reduce-scatter.16
  917.9 413.9 reduce-scatter.14
  1334.8 14.5 reduce-scatter.18
  1352.0 14.5 reduce-scatter.20
  1372.3 621.2 all-reduce.7
where the time goes:
time: 2080 us; the launch traced here: 2070 us
  waiting for transfers between devices  1770 us (85%)
  other arithmetic  101 us (5%)
  matrix products  91.4 us (4%)
  blocking collectives  74 us (4%)
    psum x1, waiting for transfers between devices, body(): lax.psum((parts[0], parts[1], parts[2], parts[3], parts[4], parts[5]), ('...  560 us
    reduce_scatter x1, waiting for transfers between devices, body(): lax.psum_scatter(grad_gate_up, 'shard', scatter_dimension=1, tiled=True)  416 us
    all_gather x1, waiting for transfers between devices, body(): lax.all_gather(gate_up, 'shard', axis=1, tiled=True)  224 us
    reduce_scatter x1, waiting for transfers between devices, body(): lax.psum_scatter(grad_down, 'shard', scatter_dimension=1, tiled=True)  215 us
    reduce_scatter x1, waiting for transfers between devices, body(): lax.psum_scatter(grad_in, 'shard', scatter_dimension=0, tiled=True)  121 us
    all_gather x1, waiting for transfers between devices, body(): lax.all_gather(down_proj, 'shard', axis=1, tiled=True)  104 us
    sub x6, other arithmetic, adamw(): weight_new = weight - step_rate * (adam_ratio + decay_factor * weight)  73.7 us
    all_gather x1, waiting for transfers between devices, body(): lax.all_gather(in_proj, 'shard', axis=0, tiled=True)  72.8 us
  transfers between devices with their start and end apart: 13, of which 12 were waited for; matrix products, arithmetic and copies ran while one was open for 5% of the time, Pallas kernels for 0%

commit v1 on v0

--- a/solution.py
+++ b/solution.py
@@ -1,13 +1,13 @@
+import functools
+
 import jax
 import jax.numpy as jnp
 from jax import lax
+from jax.experimental import pallas as pl
+from jax.experimental.pallas import tpu as pltpu
 from jax.sharding import PartitionSpec as P
 
-D = 1024
-FF = 4608
 STEP = 10
-
-
 norm_eps = 1e-05
 beta_one = 0.9
 beta_two = 0.95
@@ -15,26 +15,783 @@
 decay_rate = 0.1
 small_rate = 0.4
 
-
-def shifted(block, axis, distance):
-    devices = range(lax.axis_size(axis))
-    route = [(i - distance, i) for i in devices if i - distance in devices]
-    return lax.ppermute(block, axis, route)
-
-
-def norm_forward(values, gain_vector):
-    norm_scale = lax.rsqrt(jnp.mean(values * values, axis=-1, keepdims=True) + norm_eps)
-    unit_rows = values * norm_scale
-    return (unit_rows, norm_scale, (unit_rows * gain_vector).astype(jnp.bfloat16))
-
-
-def norm_backward(grad_normed, unit_rows, norm_scale, gain_vector):
-    gain_grad = jnp.sum(grad_normed * unit_rows, axis=(0, 1))
-    grad_unit = grad_normed * gain_vector
-    grad_values = norm_scale * (
-        grad_unit - unit_rows * jnp.mean(grad_unit * unit_rows, axis=-1, keepdims=True)
-    )
-    return (gain_grad, grad_values)
+BF = jnp.bfloat16
+F32 = jnp.float32
+MESH = pl.DeviceIdType.MESH
+CHUNK = 64
+LAGS = (0, 2, 4, 6, 9)
+PARTS = {"in": 1, "out": 1, "gate": 2, "up": 2, "down": 4}
+TILE = 16
+
+NAMES = (
+    "small", "in_0", "out_0", "gate_0", "gate_1", "up_0", "up_1", "down_0", "down_1", "down_2", "down_3",
+    "in_0_z", "out_0_z", "gate_0_z", "gate_1_z", "up_0_z", "up_1_z", "down_0_z", "down_1_z", "down_2_z",
+    "down_3_z", "n1_c", "n1_y", "n1_f", "n2_c", "n2_y", "n2_f", "ct_c", "ct_y", "ct_f", "ml_c", "ml_y",
+    "ml_f", "ro_0", "ro_1", "ro_y", "rg_0", "rg_1", "rg_y", "rr_0", "rr_1", "rr_y", "ri_0", "ri_1", "ri_y",
+    "sg_x", "sg_c", "sg_y", "sg_a", "sg_b", "sg_t",
+)
+LOCALS = (
+    "tok", "small", "ct", "in", "out", "gate", "up", "down",
+)
+
+
+def dot(a, b):
+    return lax.dot_general(a, b, (((1,), (0,)), ((), ())), preferred_element_type=F32)
+
+
+def dot_nt(a, b):
+    return lax.dot_general(a, b, (((1,), (1,)), ((), ())), preferred_element_type=F32)
+
+
+def dot_tn(a, b):
+    return lax.dot_general(a, b, (((0,), (0,)), ((), ())), preferred_element_type=F32)
+
+
+def block_kernel(
+    dims,
+    tok_h, cot_h, in_h, out_h, gu_h, dn_h, small_h,
+    block_out, token_grad, grads, small_grads,
+    WG, WD, WIN, WOUT, SM, TOK, N1, N2, CT, ML,
+    PROJ, MX, CONV, GATED, GCO, ACT, FA, GS, GO, RX,
+    MID, GM, P32, SC, RC, SY, RY, SG,
+    ss, rs, ls, xs, xr, z1s, z1r, z2s, z2r, ts, tr, ys, yr, c1s, c1r, c2s, c2r, gl,
+    ready_w, ready_a,
+):
+    D, T, FQ, F = dims
+    H, Q, R = D // 2, FQ // 2, 4 * T
+    MT = H // 2
+    NCH = 2 * D // CHUNK
+    z = lax.axis_index("rep")
+    s = lax.axis_index("seq")
+    x = lax.axis_index("shard")
+    y, c = s // 2, s % 2
+    h = z % 2
+    is_mid = jnp.logical_and(z > 0, z < 3)
+    is_end = jnp.logical_or(z == 0, z == 3)
+    xo = 1 - x
+    xp = (z, s, xo)
+    cp = (z, 2 * y + 1 - c, x)
+    yp = (z, 2 * (1 - y) + c, x)
+    zp = (z + 1 - 2 * h, s, x)
+    mp = (3 - z, s, x)
+
+    def block(i):
+        return 2 * (y + (i // 2) * (1 - 2 * y)) + c + (i % 2) * (1 - 2 * c)
+
+    def rows(m, n=T):
+        return pl.ds(pl.multiple_of(m * n, n), n)
+
+    def at(start, size, unit):
+        return pl.ds(pl.multiple_of(start, unit), size)
+
+    def remote(name, src, dst, dev):
+        k = NAMES.index(name)
+        return pltpu.make_async_remote_copy(
+            src_ref=src, dst_ref=dst, send_sem=ss.at[k], recv_sem=rs.at[k], device_id=dev, device_id_type=MESH
+        )
+
+    def local(name, src, dst):
+        return pltpu.make_async_copy(src, dst, ls.at[LOCALS.index(name)])
+
+    barrier = pltpu.get_barrier_semaphore()
+    for dev in (xp, cp, yp, zp):
+        pl.semaphore_signal(barrier, inc=1, device_id=dev, device_id_type=MESH)
+
+    @pl.when(is_mid)
+    def _():
+        pl.semaphore_signal(barrier, inc=1, device_id=mp, device_id_type=MESH)
+
+    loads = [
+        local("tok", tok_h, TOK),
+        local("small", small_h, SM.at[x]),
+        local("ct", cot_h, CT.at[rows(s)]),
+    ]
+    for j in range(3):
+        for k in range(2):
+            loads.append(
+                local(
+                    "in",
+                    in_h.at[:, at(D * j + H * k + Q * s, Q, Q)],
+                    WIN.at[rows(x, H), pl.ds(FQ * j + Q * k, Q)],
+                )
+            )
+    loads.append(local("out", out_h.at[rows(s, Q)], WOUT.at[rows(x, Q)]))
+    for j, name in enumerate(("gate", "up")):
+        loads.append(
+            local(name, gu_h.at[j, :, at(F * s, F, 128)], WG.at[at(D * j + H * x, H, H)])
+        )
+    loads.append(local("down", dn_h.at[rows(s, F)], WD.at[:, at(H * x, H, H)]))
+    for copy in loads:
+        copy.start()
+
+    def local_wait(name):
+        whole = {
+            "tok": lambda: local("tok", tok_h, TOK),
+            "small": lambda: local("small", small_h, SM.at[x]),
+            "ct": lambda: local("ct", cot_h, CT.at[rows(s)]),
+            "in": lambda: local("in", WIN.at[rows(x, H)], WIN.at[rows(x, H)]),
+            "out": lambda: local("out", WOUT.at[rows(x, Q)], WOUT.at[rows(x, Q)]),
+            "gate": lambda: local("gate", WG.at[at(H * x, H, H)], WG.at[at(H * x, H, H)]),
+            "up": lambda: local("up", WG.at[at(D + H * x, H, H)], WG.at[at(D + H * x, H, H)]),
+            "down": lambda: local("down", WD.at[:, at(H * x, H, H)], WD.at[:, at(H * x, H, H)]),
+        }
+        whole[name]().wait()
+
+    @pl.when(is_mid)
+    def _():
+        pl.semaphore_wait(barrier, 5)
+
+    @pl.when(is_end)
+    def _():
+        pl.semaphore_wait(barrier, 4)
+
+    def part(name, owner, half, p):
+        if name == "in":
+            return WIN.at[at(H * owner + (H // 2) * half, H // 2, H // 2)]
+        if name == "out":
+            return WOUT.at[at(Q * owner + (Q // 2) * half, Q // 2, Q // 2)]
+        if name == "down":
+            n = F // 2 // PARTS[name]
+            return WD.at[at((F // 2) * half + n * p, n, 16), at(H * owner, H, H)]
+        j = 0 if name == "gate" else 1
+        n = H // 2 // PARTS[name]
+        return WG.at[at(D * j + H * owner + (H // 2) * half + n * p, n, n)]
+
+    def weight_send(name):
+        if name == "in":
+            for j in range(3):
+                for k in range(2):
+                    remote(
+                        "in_0",
+                        in_h.at[at((H // 2) * h, H // 2, H // 2), at(D * j + H * k + Q * s, Q, Q)],
+                        WIN.at[at(H * x + (H // 2) * h, H // 2, H // 2), pl.ds(FQ * j + Q * k, Q)],
+                        xp,
+                    ).start()
+            return
+        for p in range(PARTS[name]):
+            if name == "out":
+                src = out_h.at[at(Q * s + (Q // 2) * h, Q // 2, Q // 2)]
+            elif name == "down":
+                n = F // 2 // PARTS[name]
+                src = dn_h.at[at(F * s + (F // 2) * h + n * p, n, 16)]
+            else:
+                n = H // 2 // PARTS[name]
+                src = gu_h.at[0 if name == "gate" else 1, at((H // 2) * h + n * p, n, n), at(F * s, F, 128)]
+            remote(name + "_" + str(p), src, part(name, x, h, p), xp).start()
+
+    def weight_pass(name):
+        for p in range(PARTS[name]):
+            here = part(name, xo, h, p)
+            remote(name + "_" + str(p), here, here, xp).wait_recv()
+            remote(name + "_" + str(p) + "_z", here, here, zp).start()
+
+    def weight_wait(name):
+        local_wait(name)
+        for p in range(PARTS[name]):
+            there = part(name, xo, 1 - h, p)
+            remote(name + "_" + str(p) + "_z", there, there, zp).wait_recv()
+
+    def weight_sent(name):
+        for p in range(PARTS[name]):
+            here = part(name, x, h, p)
+            remote(name + "_" + str(p), here, here, xp).wait_send()
+
+    def weight_passed(name):
+        for p in range(PARTS[name]):
+            here = part(name, xo, h, p)
+            remote(name + "_" + str(p) + "_z", here, here, zp).wait_send()
+
+    remote("small", small_h, SM.at[x], xp).start()
+    weight_send("in")
+    weight_send("out")
+    weight_send("gate")
+    weight_send("up")
+    weight_send("down")
+
+    def gather_copy(name, buf, kind):
+        m = block(2) if kind == "f" else s
+        return remote(name + "_" + kind, buf.at[rows(m)], buf.at[rows(m)], yp if kind == "y" else cp)
+
+    def gather_start(name, buf):
+        gather_copy(name, buf, "y").start()
+        gather_copy(name, buf, "c").start()
+
+    def gather_step(name, buf, i):
+        @pl.when(i == 1)
+        def _():
+            remote(name + "_c", buf.at[rows(block(1))], buf.at[rows(block(1))], cp).wait_recv()
+
+        @pl.when(i == 2)
+        def _():
+            remote(name + "_y", buf.at[rows(block(2))], buf.at[rows(block(2))], yp).wait_recv()
+            gather_copy(name, buf, "f").start()
+
+        @pl.when(i == 3)
+        def _():
+            remote(name + "_f", buf.at[rows(block(3))], buf.at[rows(block(3))], cp).wait_recv()
+
+    def sum_core(name, lot, k):
+        return remote(name + "_" + str(k), SC.at[lot, k], RC.at[lot, k], cp)
+
+    def sum_y(name, lot):
+        return remote(name + "_y", SY.at[lot], RY.at[lot], yp)
+
+    def sum_emit(name, lot, i, partial):
+        @pl.when(i % 2 == 0)
+        def _():
+            P32[i // 2] = partial
+
+        @pl.when(i == 1)
+        def _():
+            SC[lot, 1] = partial.astype(BF)
+            sum_core(name, lot, 1).start()
+
+        @pl.when(i == 3)
+        def _():
+            SC[lot, 0] = partial.astype(BF)
+            sum_core(name, lot, 0).start()
+
+    def sum_cross(name, lot):
+        sum_core(name, lot, 0).wait_recv()
+        SY[lot] = (P32[1] + RC[lot, 0].astype(F32)).astype(BF)
+        sum_y(name, lot).start()
+
+    def sum_wait(name, lot):
+        sum_core(name, lot, 1).wait_recv()
+        sum_y(name, lot).wait_recv()
+
+    def sum_rows(lot, r):
+        return P32[0, r] + RC[lot, 1, r].astype(F32) + RY[lot, r].astype(F32)
+
+    def sum_done(name, lot):
+        sum_core(name, lot, 0).wait_send()
+        sum_core(name, lot, 1).wait_send()
+        sum_y(name, lot).wait_send()
+
+    def tiles(n, body, size=TILE):
+        def step(t, carry):
+            body(pl.ds(pl.multiple_of(t * size, size), size))
+            return carry
+
+        lax.fori_loop(0, n // size, step, 0)
+
+    def blocks(body, first=0, last=4):
+        def step(i, carry):
+            body(i, block(i))
+            return carry
+
+        lax.fori_loop(first, last, step, 0)
+
+    def gain(k):
+        return jnp.concatenate([SM[0, 3 + k : 4 + k, :], SM[1, 3 + k : 4 + k, :]], axis=1)
+
+    def tap(k):
+        cols = rows(s, Q)
+        return jnp.concatenate([SM[0, k : k + 1, cols], SM[1, k : k + 1, cols]], axis=1)
+
+    local_wait("tok")
+    local_wait("small")
+    remote("small", small_h, SM.at[xo], xp).wait()
+    SG[0] = jnp.zeros_like(SG[0])
+
+    gain_one = gain(0)
+
+    def norm_one(r):
+        v = TOK[r].astype(F32)
+        scale = lax.rsqrt(jnp.mean(v * v, axis=-1, keepdims=True) + norm_eps)
+        N1[pl.ds(pl.multiple_of(s * T + r.start, TILE), TILE)] = (v * scale * gain_one).astype(BF)
+
+    tiles(T, norm_one)
+    gather_start("n1", N1)
+    local_wait("ct")
+    gather_start("ct", CT)
+
+    MX[0:8] = jnp.zeros((8, FQ), F32)
+    GCO[R : R + 8] = jnp.zeros((8, FQ), F32)
+    weight_pass("in")
+    weight_pass("out")
+    weight_wait("in")
+
+    def project(i, m):
+        gather_step("n1", N1, i)
+        p = dot(N1[rows(m)], WIN[...])
+        PROJ[rows(m)] = p
+        mixed = (p[:, :FQ] * p[:, 2 * FQ :]).astype(BF)
+        MX[at(8 + m * T, T, 8)] = mixed.astype(F32)
+
+    blocks(project)
+    weight_wait("out")
+
+    def convolve(i, m):
+        i = 3 - i
+        m = block(i)
+        ext = MX[at(m * T, T + 8, 8)]
+        conv = tap(0) * ext[6 : 6 + T] + tap(1) * ext[7 : 7 + T] + tap(2) * ext[8 : 8 + T]
+        CONV[rows(m)] = conv
+        gated = (PROJ[rows(m), FQ : 2 * FQ] * conv).astype(BF)
+        GATED[rows(m)] = gated
+        sum_emit("ro", 0, i, dot(gated, WOUT[...]))
+
+    blocks(convolve)
+    sum_cross("ro", 0)
+    weight_pass("gate")
+    sum_wait("ro", 0)
+
+    gain_two = gain(1)
+
+    def norm_two(r):
+        v = TOK[r].astype(F32) + sum_rows(0, r)
+        MID[r] = v
+        scale = lax.rsqrt(jnp.mean(v * v, axis=-1, keepdims=True) + norm_eps)
+        N2[pl.ds(pl.multiple_of(s * T + r.start, TILE), TILE)] = (v * scale * gain_two).astype(BF)
+
+    tiles(T, norm_two)
+    gather_start("n2", N2)
+    sum_done("ro", 0)
+    weight_pass("up")
+    weight_pass("down")
+    weight_wait("gate")
+    weight_wait("up")
+    weight_wait("down")
+
+    def feed(i, m):
+        gather_step("n2", N2, i)
+        gather_step("ct", CT, i)
+        FA[0] = dot(N2[rows(m)], WG[0:D])
+        FA[1] = dot(N2[rows(m)], WG[D : 2 * D])
+        FA[2] = dot_nt(CT[rows(m)], WD[...])
+
+        def act(r):
+            gate, up, gh = FA[0, r], FA[1, r], FA[2, r]
+            sig = jax.nn.sigmoid(gate)
+            silu = gate * sig
+            ro = pl.ds(pl.multiple_of(m * T + r.start, TILE), TILE)
+            ACT[ro] = (gh * up * sig * (1.0 + gate * (1.0 - sig))).astype(BF)
+            ro = pl.ds(pl.multiple_of(R + m * T + r.start, TILE), TILE)
+            ACT[ro] = (gh * silu).astype(BF)
+            ro = pl.ds(pl.multiple_of(2 * R + m * T + r.start, TILE), TILE)
+            ACT[ro] = (silu * up).astype(BF)
+
+        tiles(T, act)
+        partial = dot_nt(ACT[rows(m)], WG[0:D]) + dot_nt(ACT[at(R + m * T, T, T)], WG[D : 2 * D])
+        sum_emit("rg", 1, i, partial)
+
+    blocks(feed)
+    sum_cross("rg", 1)
+    weight_passed("gate")
+    weight_passed("up")
+    pl.semaphore_signal(ready_w, inc=1, device_id=zp, device_id_type=MESH)
+
+    def chunk(k):
+        return rows(k, CHUNK)
+
+    def x_copy(k):
+        return pltpu.make_async_remote_copy(
+            src_ref=GS.at[chunk(k)], dst_ref=RX.at[chunk(k)], send_sem=xs.at[k], recv_sem=xr.at[k],
+            device_id=xp, device_id_type=MESH,
+        )
+
+    def z1_copy(k):
+        return pltpu.make_async_remote_copy(
+            src_ref=GO.at[chunk(k)], dst_ref=WG.at[chunk(k)], send_sem=z1s.at[k], recv_sem=z1r.at[k],
+            device_id=zp, device_id_type=MESH,
+        )
+
+    def z2_copy(k):
+        return pltpu.make_async_remote_copy(
+            src_ref=RX.at[chunk(k)], dst_ref=ACT.at[chunk(k)], send_sem=z2s.at[k], recv_sem=z2r.at[k],
+            device_id=mp, device_id_type=MESH,
+        )
+
+    def t_copy(k):
+        return pltpu.make_async_remote_copy(
+            src_ref=GO.at[chunk(k)], dst_ref=WG.at[chunk(k)], send_sem=ts.at[k], recv_sem=tr.at[k],
+            device_id=zp, device_id_type=MESH,
+        )
+
+    def y_copy(k, src):
+        return pltpu.make_async_remote_copy(
+            src_ref=src.at[chunk(k)], dst_ref=grads.at[s, chunk(k)], send_sem=ys.at[k], recv_sem=yr.at[k],
+            device_id=yp, device_id_type=MESH,
+        )
+
+    def c1_copy(k, src):
+        return pltpu.make_async_remote_copy(
+            src_ref=src.at[chunk(k)], dst_ref=grads.at[s, chunk(k)], send_sem=c1s.at[k], recv_sem=c1r.at[k],
+            device_id=cp, device_id_type=MESH,
+        )
+
+    def c2_copy(k):
+        m = block(2)
+        return pltpu.make_async_remote_copy(
+            src_ref=grads.at[m, chunk(k)], dst_ref=grads.at[m, chunk(k)], send_sem=c2s.at[k], recv_sem=c2r.at[k],
+            device_id=cp, device_id_type=MESH,
+        )
+
+    def own_copy(k, src):
+        return pltpu.make_async_copy(src.at[chunk(k)], grads.at[s, chunk(k)], gl.at[k])
+
+    def add_rows(k, dst, one, two):
+        def step(t, carry):
+            r = pl.ds(pl.multiple_of(k * CHUNK + t * TILE, TILE), TILE)
+            dst[r] = (one[r].astype(F32) + two[r].astype(F32)).astype(BF)
+            return carry
+
+        lax.fori_loop(0, CHUNK // TILE, step, 0)
+
+    def tick(k):
+        def stage(lag, body):
+            pl.when(jnp.logical_and(k >= lag, k < NCH + lag))(lambda: body(k - lag))
+
+        def add_x(k):
+            x_copy(k).wait_recv()
+            add_rows(k, GO, GO, RX)
+            pl.when(is_end)(lambda: z1_copy(k).start())
+
+        def add_end(k):
+            @pl.when(is_mid)
+            def _():
+                z1_copy(k).wait_recv()
+                add_rows(k, RX, GO, WG)
+                z2_copy(k).start()
+
+        def spread(k, src):
+            y_copy(k, src).start()
+            c1_copy(k, src).start()
+            own_copy(k, src).start()
+
+        def add_mid(k):
+            @pl.when(is_mid)
+            def _():
+                z2_copy(k).wait_recv()
+                add_rows(k, GO, RX, ACT)
+                t_copy(k).start()
+                spread(k, GO)
+
+        def take(k):
+            @pl.when(is_end)
+            def _():
+                t_copy(k).wait_recv()
+                spread(k, WG)
+
+        def hand(k):
+            m = block(2)
+            pltpu.make_async_remote_copy(
+                src_ref=grads.at[m, chunk(k)], dst_ref=grads.at[m, chunk(k)], send_sem=ys.at[k], recv_sem=yr.at[k],
+                device_id=yp, device_id_type=MESH,
+            ).wait_recv()
+            c2_copy(k).start()
+
+        for body, lag in zip((add_x, add_end, add_mid, take, hand), LAGS):
+            stage(lag, body)
+
+    def ticks(first, last):
+        def step(k, carry):
+            tick(k)
+            return carry
+
+        lax.fori_loop(first, last, step, 0)
+
+    def weight_grad(row, left, right, cols, dst, owner):
+        def step(t, carry):
+            lhs = left[:, at(H * owner + MT * t, MT, MT)]
+            dst[at(row + MT * t, MT, MT), 0:cols] = dot_tn(lhs, right()).astype(BF)
+            return carry
+
+        lax.fori_loop(0, H // MT, step, 0)
+
+    def act_at(j):
+        return lambda: ACT[j * R : (j + 1) * R]
+
+    def send(first, last):
+        for k in range(first, last):
+            x_copy(k).start()
+
+    n_arr = H // CHUNK
+    weight_grad(0, N2, act_at(0), F, GS, xo)
+    send(0, n_arr)
+    weight_grad(H, N2, act_at(1), F, GS, xo)
+    send(n_arr, 2 * n_arr)
+    weight_grad(2 * H, CT, act_at(2), F, GS, xo)
+    send(2 * n_arr, 3 * n_arr)
+    weight_grad(0, N2, act_at(0), F, GO, x)
+    weight_grad(H, N2, act_at(1), F, GO, x)
+    weight_grad(2 * H, CT, act_at(2), F, GO, x)
+
+    @pl.when(is_mid)
+    def _():
+        pl.semaphore_signal(ready_a, inc=1, device_id=mp, device_id_type=MESH)
+
+    pl.semaphore_wait(ready_w, 1)
+
+    @pl.when(is_mid)
+    def _():
+        pl.semaphore_wait(ready_a, 1)
+
+    ticks(0, 3)
+
+    sum_wait("rg", 1)
+
+    def back_two(t, acc):
+        r = pl.ds(pl.multiple_of(t * TILE, TILE), TILE)
+        v = MID[r]
+        scale = lax.rsqrt(jnp.mean(v * v, axis=-1, keepdims=True) + norm_eps)
+        unit = v * scale
+        e = sum_rows(1, r)
+        eu = e * unit
+        ew = e * gain_two
+        grad = scale * (ew - unit * jnp.mean(ew * unit, axis=-1, keepdims=True))
+        ro = pl.ds(pl.multiple_of(s * T + t * TILE, TILE), TILE)
+        gm = CT[ro].astype(F32) + grad
+        GM[r] = gm
+        ML[ro] = gm.astype(BF)
+        return acc + jnp.sum(eu, axis=0, keepdims=True)
+
+    SG[0, 4:5, :] = lax.fori_loop(0, T // TILE, back_two, jnp.zeros((1, D), F32))
+    gather_start("ml", ML)
+    sum_done("rg", 1)
+    ticks(3, 7)
+
+    def gated_back(i, m):
+        gather_step("ml", ML, i)
+        gg = dot_nt(ML[rows(m)], WOUT[...])
+        gco = gg * PROJ[rows(m), FQ : 2 * FQ]
+        GCO[rows(m)] = gco
+        PROJ[rows(m), FQ : 2 * FQ] = gg * CONV[rows(m)]
+
+    blocks(gated_back)
+    for kind in "cyf":
+        gather_copy("n2", N2, kind).wait_send()
+
+    def conv_back(i, acc):
+        m = block(i)
+        gco = GCO[at(m * T, T + 8, 8)]
+        ext = MX[at(m * T, T + 8, 8)]
+        here = gco[0:T]
+        gm = tap(2) * here + tap(1) * gco[1 : 1 + T] + tap(0) * gco[2 : 2 + T]
+        p = PROJ[rows(m)]
+        low = jnp.concatenate([gm * p[:, 2 * FQ :], p[:, FQ : 2 * FQ], gm * p[:, :FQ]], axis=1).astype(BF)
+        N2[rows(m), 0 : 3 * FQ] = low
+        sum_emit("ri", 1, i, dot_nt(low, WIN[...]))
+        return tuple(
+            a + jnp.sum(here * ext[6 + k : 6 + k + T], axis=0, keepdims=True) for k, a in enumerate(acc)
+        )
+
+    def conv_step(i, acc):
+        return conv_back(3 - i, acc)
+
+    conv_grads = lax.fori_loop(0, 4, conv_step, (jnp.zeros((1, FQ), F32),) * 3)
+    for k in range(3):
+        SG[0, k : k + 1, rows(s, Q)] = conv_grads[k][:, :Q]
+        SG[0, k : k + 1, at(H + s * Q, Q, Q)] = conv_grads[k][:, Q:]
+    sum_cross("ri", 1)
+
+    def io_grad(dst, owner):
+        def step(t, carry):
+            lhs = N1[:, at(H * owner + MT * t, MT, MT)]
+            dst[at(3 * H + MT * t, MT, MT), 0 : 3 * FQ] = dot_tn(lhs, N2[:, 0 : 3 * FQ]).astype(BF)
+            right = GATED[:, rows(owner, Q)]
+            for j in range(2):
+                lhs = ML[:, at(H * j + MT * t, MT, MT)]
+                dst[at(3 * H + MT * t, MT, MT), 3 * FQ + Q * j : 3 * FQ + Q * (j + 1)] = dot_tn(lhs, right).astype(BF)
+            if 3 * FQ + 2 * Q < F:
+                dst[at(3 * H + MT * t, MT, MT), 3 * FQ + 2 * Q : F] = jnp.zeros((MT, F - 3 * FQ - 2 * Q), BF)
+            return carry
+
+        lax.fori_loop(0, H // MT, step, 0)
+
+    io_grad(GS, xo)
+    send(3 * n_arr, NCH)
+    ticks(7, 9)
+    io_grad(GO, x)
+    ticks(9, 11)
+
+    sum_wait("ri", 1)
+    TOKOUT = SC.at[0, 0]
+
+    def back_one(t, acc):
+        r = pl.ds(pl.multiple_of(t * TILE, TILE), TILE)
+        v = TOK[r].astype(F32)
+        scale = lax.rsqrt(jnp.mean(v * v, axis=-1, keepdims=True) + norm_eps)
+        unit = v * scale
+        e = sum_rows(1, r)
+        eu = e * unit
+        ew = e * gain_one
+        grad = scale * (ew - unit * jnp.mean(ew * unit, axis=-1, keepdims=True))
+        TOKOUT[r] = (GM[r] + grad).astype(BF)
+        return acc + jnp.sum(eu, axis=0, keepdims=True)
+
+    SG[0, 3:4, :] = lax.fori_loop(0, T // TILE, back_one, jnp.zeros((1, D), F32))
+    out_copy = pltpu.make_async_copy(TOKOUT, token_grad, ls.at[LOCALS.index("tok")])
+    out_copy.start()
+    sum_done("ri", 1)
+    ticks(11, 13)
+
+    out_copy.wait()
+
+    def down(i, m):
+        i = 3 - i
+        m = block(i)
+        sum_emit("rr", 0, i, dot(ACT[at(2 * R + m * T, T, T)], WD[...]))
+
+    blocks(down)
+    sum_cross("rr", 0)
+
+    def small_start(name, dev, k):
+        remote(name, SG.at[0], SG.at[k], dev).start()
+
+    def small_end(name, dev, k):
+        remote(name, SG.at[0], SG.at[k], dev).wait()
+        SG[0] = SG[0] + SG[k]
+
+    small_start("sg_x", xp, 1)
+    ticks(13, 15)
+    small_end("sg_x", xp, 1)
+    small_start("sg_c", cp, 2)
+    ticks(15, 16)
+    small_end("sg_c", cp, 2)
+    small_start("sg_y", yp, 3)
+    ticks(16, 19)
+    small_end("sg_y", yp, 3)
+    pl.when(is_end)(lambda: small_start("sg_a", zp, 4))
+    ticks(19, 20)
+
+    sum_wait("rr", 0)
+    sum_done("rr", 0)
+
+    def result(r):
+        TOKOUT[r] = (MID[r] + sum_rows(0, r)).astype(BF)
+
+    tiles(T, result)
+    out_copy = pltpu.make_async_copy(TOKOUT, block_out, ls.at[LOCALS.index("tok")])
+    out_copy.start()
+    ticks(20, 22)
+
+    @pl.when(is_mid)
+    def _():
+        remote("sg_a", SG.at[0], SG.at[4], zp).wait_recv()
+        SG[0] = SG[0] + SG[4]
+        small_start("sg_b", mp, 5)
+
+    ticks(22, 25)
+
+    @pl.when(is_end)
+    def _():
+        remote("sg_a", SG.at[0], SG.at[4], zp).wait_send()
+
+    @pl.when(is_mid)
+    def _():
+        remote("sg_b", SG.at[0], SG.at[5], mp).wait()
+        SG[6] = SG[0] + SG[5]
+        remote("sg_t", SG.at[6], SG.at[6], zp).start()
+
+    ticks(25, 30)
+
+    @pl.when(is_mid)
+    def _():
+        remote("sg_t", SG.at[6], SG.at[6], zp).wait_send()
+
+    @pl.when(is_end)
+    def _():
+        remote("sg_t", SG.at[6], SG.at[6], zp).wait_recv()
+
+    small_copy = pltpu.make_async_copy(SG.at[6], small_grads, ls.at[LOCALS.index("small")])
+    small_copy.start()
+    ticks(30, NCH + LAGS[-1])
+
+    def finish(k, carry):
+        x_copy(k).wait_send()
+
+        @pl.when(is_end)
+        def _():
+            z1_copy(k).wait_send()
+
+        @pl.when(is_mid)
+        def _():
+            z2_copy(k).wait_send()
+            t_copy(k).wait_send()
+
+        y_copy(k, GO).wait_send()
+        c1_copy(k, GO).wait()
+        c2_copy(k).wait()
+        own_copy(k, GO).wait()
+        return carry
+
+    lax.fori_loop(0, NCH, finish, 0)
+    out_copy.wait()
+    small_copy.wait()
+    for name in ("in", "out", "gate", "up", "down"):
+        weight_sent(name)
+        if name not in ("gate", "up"):
+            weight_passed(name)
+    for name, buf in (("n1", N1), ("ct", CT), ("ml", ML)):
+        for kind in "cyf":
+            gather_copy(name, buf, kind).wait_send()
+
+
+def run_block(tokens, cotangent, in_proj, out_proj, gate_up, down_proj, small):
+    T, D = tokens.shape
+    F = gate_up.shape[2] // 4
+    FQ = D // 4
+    R = 4 * T
+    dims = (D, T, FQ, F)
+    NCH = 2 * D // CHUNK
+    hbm = pl.BlockSpec(memory_space=pltpu.HBM)
+    dma = pltpu.SemaphoreType.DMA
+    vmem = pltpu.VMEM
+    scratch = [
+        vmem((2 * D, F), BF),
+        vmem((F, D), BF),
+        vmem((D, 3 * FQ), BF),
+        vmem((FQ, D), BF),
+        vmem((2, 8, D // 2), F32),
+        vmem((T, D), BF),
+        vmem((R, D), BF),
+        vmem((R, D), BF),
+        vmem((R, D), BF),
+        vmem((R, D), BF),
+        vmem((R, 3 * FQ), F32),
+        vmem((R + 8, FQ), F32),
+        vmem((R, FQ), F32),
+        vmem((R, FQ), BF),
+        vmem((R + 8, FQ), F32),
+        vmem((3 * R, F), BF),
+        vmem((3, T, F), F32),
+        vmem((2 * D, F), BF),
+        vmem((2 * D, F), BF),
+        vmem((2 * D, F), BF),
+        vmem((T, D), F32),
+        vmem((T, D), F32),
+        vmem((2, T, D), F32),
+        vmem((2, 2, T, D), BF),
+        vmem((2, 2, T, D), BF),
+        vmem((2, T, D), BF),
+        vmem((2, T, D), BF),
+        vmem((7, 8, D), F32),
+        dma((len(NAMES),)),
+        dma((len(NAMES),)),
+        dma((len(LOCALS),)),
+    ]
+    scratch += [dma((NCH,))] * 15
+    scratch += [pltpu.SemaphoreType.REGULAR, pltpu.SemaphoreType.REGULAR]
+    flops = 6 * R * D * (3 * F + 4 * FQ) * 2
+    return pl.pallas_call(
+        functools.partial(block_kernel, dims),
+        out_shape=(
+            jax.ShapeDtypeStruct((T, D), BF),
+            jax.ShapeDtypeStruct((T, D), BF),
+            jax.ShapeDtypeStruct((4, 2 * D, F), BF),
+            jax.ShapeDtypeStruct((8, D), F32),
+        ),
+        in_specs=[hbm] * 7,
+        out_specs=(hbm,) * 4,
+        scratch_shapes=scratch,
+        compiler_params=pltpu.CompilerParams(
+            collective_id=0, has_side_effects=True, vmem_limit_bytes=62 * 2**20
+        ),
+        cost_estimate=pl.CostEstimate(flops=flops, bytes_accessed=60 * 2**20, transcendentals=R * F),
+        name="block_kernel",
+    )(tokens, cotangent, in_proj, out_proj, gate_up, down_proj, small)
 
 
 def adamw(weight, first_moment, second_moment, gradient, step_rate, decay_factor):
@@ -49,7 +806,130 @@
     return (weight_new, first_new, second_new)
 
 
-def body(
+def update_values(rate, w, m, v, grad):
+    return adamw(w.astype(F32), m.astype(F32), v.astype(F32), grad.astype(F32), rate, decay_rate)
+
+
+def update_plain(rate, w, m, v, g, *new):
+    shape = w.shape
+    flat = shape[-2:]
+    values = update_values(rate, w[...].reshape(flat), m[...].reshape(flat), v[...].reshape(flat), g[...].reshape(flat))
+    for ref, value in zip(new, values):
+        ref[...] = value.reshape(shape)
+
+
+def update_turned(rate, w, m, v, g, *new):
+    values = update_values(rate, w[...], m[...], v[...], g[0].astype(F32).T)
+    for ref, value in zip(new, values):
+        ref[...] = value
+
+
+def update_inner(rate, w, m, v, g, *new):
+    n = g.shape[0]
+    Q = w.shape[1] // (6 * n)
+    for j in range(6):
+        for k in range(n):
+            cols = slice((n * j + k) * Q, (n * j + k + 1) * Q)
+            values = update_values(rate, w[:, cols], m[:, cols], v[:, cols], g[k, :, Q * j : Q * (j + 1)])
+            for ref, value in zip(new, values):
+                ref[:, cols] = value
+
+
+def update_outer(rate, w, m, v, g, *new):
+    H, Q = g.shape[1], g.shape[2] // 2
+    for j in range(2):
+        cols = slice(H * j, H * (j + 1))
+        grad = g[0, :, Q * j : Q * (j + 1)].astype(F32).T
+        values = update_values(rate, w[:, cols], m[:, cols], v[:, cols], grad)
+        for ref, value in zip(new, values):
+            ref[:, cols] = value
+
+
+def update(kernel, weight, first, second, grads, rate, grid, block, at, g_block, g_at, name):
+    spec = pl.BlockSpec(block, at)
+    n = weight.size
+    return pl.pallas_call(
+        functools.partial(kernel, rate),
+        grid=grid,
+        in_specs=[spec, spec, spec, pl.BlockSpec(g_block, g_at)],
+        out_specs=(spec,) * 3,
+        out_shape=(jax.ShapeDtypeStruct(weight.shape, F32),) * 3,
+        compiler_params=pltpu.CompilerParams(vmem_limit_bytes=56 * 2**20),
+        cost_estimate=pl.CostEstimate(flops=12 * n, bytes_accessed=20 * n, transcendentals=2 * n),
+        name=name,
+    )(weight, first, second, grads)
+
+
+def fused_body(
+    tokens, cotangent, in_proj, in_moment, in_square, out_proj, out_moment, out_square,
+    gate_up, gate_moment, gate_square, down_proj, down_moment, down_square,
+    conv_kernel, conv_moment, conv_square, norm_gains, gains_moment, gains_square,
+):
+    T, D = tokens.shape[1:]
+    H, Q = D // 2, D // 8
+    F = gate_up.shape[2] // 4
+    FF = 4 * F
+    rate = 2.0 * D ** (-0.5)
+    down_rate = 2.0 * FF ** (-0.5)
+    small = jnp.concatenate(
+        [conv_kernel.astype(F32), norm_gains.astype(F32), jnp.zeros((3, H), F32)], axis=0
+    )
+    block_out, token_grad, grads, small_grads = run_block(
+        tokens[0], cotangent[0], in_proj, out_proj, gate_up, down_proj, small
+    )
+    n = H // 256
+    gate = update(
+        update_plain, gate_up, gate_moment, gate_square, grads, rate,
+        (2, n, 4), (1, 256, F), lambda j, r, k: (j, r, k),
+        (1, 256, F), lambda j, r, k: (k, j * n + r, 0), "update_gate",
+    )
+    down = update(
+        update_turned, down_proj, down_moment, down_square, grads, down_rate,
+        (4, n), (F, 256), lambda k, r: (k, r),
+        (1, 256, F), lambda k, r: (k, 2 * n + r, 0), "update_down",
+    )
+    inner = update(
+        update_inner, in_proj, in_moment, in_square, grads, rate,
+        (H // 64,), (64, 3 * D), lambda r: (r, 0),
+        (4, 64, F), lambda r: (0, 3 * H // 64 + r, 0), "update_in",
+    )
+    outer = update(
+        update_outer, out_proj, out_moment, out_square, grads, rate,
+        (4,), (Q, D), lambda k: (k, 0),
+        (1, H, 2 * Q), lambda k: (k, 3, 3), "update_out",
+    )
+    mine = lax.dynamic_slice_in_dim(small_grads, lax.axis_index("shard") * H, H, axis=1)
+    conv = adamw(
+        conv_kernel.astype(F32), conv_moment.astype(F32), conv_square.astype(F32), mine[0:3], small_rate, 0.0
+    )
+    gains = adamw(
+        norm_gains.astype(F32), gains_moment.astype(F32), gains_square.astype(F32), mine[3:5], small_rate, 0.0
+    )
+    return (block_out[None], token_grad[None], *inner, *outer, *gate, *down, *conv, *gains)
+
+
+def shifted(block, axis, distance):
+    devices = range(lax.axis_size(axis))
+    route = [(i - distance, i) for i in devices if i - distance in devices]
+    return lax.ppermute(block, axis, route)
+
+
+def norm_forward(values, gain_vector):
+    norm_scale = lax.rsqrt(jnp.mean(values * values, axis=-1, keepdims=True) + norm_eps)
+    unit_rows = values * norm_scale
+    return (unit_rows, norm_scale, (unit_rows * gain_vector).astype(jnp.bfloat16))
+
+
+def norm_backward(grad_normed, unit_rows, norm_scale, gain_vector):
+    gain_grad = jnp.sum(grad_normed * unit_rows, axis=(0, 1))
+    grad_unit = grad_normed * gain_vector
+    grad_values = norm_scale * (
+        grad_unit - unit_rows * jnp.mean(grad_unit * unit_rows, axis=-1, keepdims=True)
+    )
+    return (gain_grad, grad_values)
+
+
+def plain_body(
     tokens,
     cotangent,
     in_proj,
@@ -183,8 +1063,8 @@
         lax.psum_scatter(grad_gains, "shard", scatter_dimension=1, tiled=True),
     )
     totals = lax.psum((parts[0], parts[1], parts[2], parts[3], parts[4], parts[5]), ("rep", "seq"))
-    matrix_rate = 2.0 * D ** (-0.5)
-    down_rate = 2.0 * FF ** (-0.5)
+    matrix_rate = 2.0 * model_width ** (-0.5)
+    down_rate = 2.0 * gate_up.shape[2] ** (-0.5)
     in_next, in_moment_next, in_square_next = adamw(
         in_proj.astype(jnp.float32),
         in_moment.astype(jnp.float32),
@@ -258,48 +1138,11 @@
 
 
 def solution(mesh):
-    in_specs = (
-        P(("rep", "shard"), "seq", None),
-        P(("rep", "shard"), "seq", None),
-        P("shard", None),
-        P("shard", None),
-        P("shard", None),
-        P("shard", None),
-        P("shard", None),
-        P("shard", None),
-        P(None, "shard", None),
-        P(None, "shard", None),
-        P(None, "shard", None),
-        P(None, "shard"),
-        P(None, "shard"),
-        P(None, "shard"),
-        P(None, "shard"),
-        P(None, "shard"),
-        P(None, "shard"),
-        P(None, "shard"),
-        P(None, "shard"),
-        P(None, "shard"),
-    )
-    out_specs = (
-        P(("rep", "shard"), "seq", None),
-        P(("rep", "shard"), "seq", None),
-        P("shard", None),
-        P("shard", None),
-        P("shard", None),
-        P("shard", None),
-        P("shard", None),
-        P("shard", None),
-        P(None, "shard", None),
-        P(None, "shard", None),
-        P(None, "shard", None),
-        P(None, "shard"),
-        P(None, "shard"),
-        P(None, "shard"),
-        P(None, "shard"),
-        P(None, "shard"),
-        P(None, "shard"),
-        P(None, "shard"),
-        P(None, "shard"),
-        P(None, "shard"),
-    )
-    return jax.shard_map(body, mesh=mesh, in_specs=in_specs, out_specs=out_specs, check_vma=False)
+    act = P(("rep", "shard"), "seq", None)
+    weights = (
+        (P("shard", None),) * 6 + (P(None, "shard", None),) * 3 + (P(None, "shard"),) * 9
+    )
+    specs = (act, act) + weights
+    sizes = (mesh.shape["rep"], mesh.shape["seq"], mesh.shape["shard"])
+    body = fused_body if sizes == (4, 4, 2) else plain_body
+    return jax.shard_map(body, mesh=mesh, in_specs=specs, out_specs=specs, check_vma=False)

time: 2080 us -> 364 us (0.17)
  waiting for transfers between devices: 1770 us -> 0 us
  Pallas kernels: 0 us -> 356 us
  other arithmetic: 101 us -> 4.76 us
  matrix products: 91.4 us -> 0 us
  blocking collectives: 74 us -> 0 us
    reduce_scatter x4 -> x0, waiting for transfers between devices: 752 us -> none  [the longest x1 416 us: body(): lax.psum_scatter(grad_gate_up, 'shard', scatter_dimension=1, tiled=True)]
    psum x1 -> x0, waiting for transfers between devices: 560 us -> none  [body(): lax.psum((parts[0], parts[1], parts[2], parts[3], parts[4], parts[5]), ('...]
    all_gather x4 -> x0, waiting for transfers between devices: 426 us -> none  [the longest x1 224 us: body(): lax.all_gather(gate_up, 'shard', axis=1, tiled=True)]
    pallas_call x0 -> x5, Pallas kernels: none -> 356 us  [the longest x1 277 us: run_block(): pl.pallas_call(functools.partial(block_kernel, dims), out_shape=(jax.Shap...]
    dot_general x15 -> x0, matrix products: 91.4 us -> none  [the longest x1 9.93 us: body(): jnp.einsum('scf,scd->fd', hidden, cotangent, preferred_element_type=jnp.f...]
    sub x6 -> x2, other arithmetic: 73.7 us -> 2.77 us  [adamw(): weight_new = weight - step_rate * (adam_ratio + decay_factor * weight)]
    psum x1 -> x0, blocking collectives: 64.4 us -> none  [body(): lax.psum((parts[0], parts[1], parts[2], parts[3], parts[4], parts[5]), ('...]
    unnamed x13 -> x0, waiting for transfers between devices: 27.3 us -> none
  transfers between devices with their start and end apart: 13 -> 0, of which waited for: 12 -> 0; matrix products, arithmetic and copies ran while one was open for 5% -> 0% of each run, Pallas kernels for 0% -> 0%
where the time goes in v1:
time: 364 us; the launch traced here: 363 us
  Pallas kernels  356 us (98%)
  other arithmetic  4.76 us (1%)
    pallas_call x1, Pallas kernels, run_block(): pl.pallas_call(functools.partial(block_kernel, dims), out_shape=(jax.Shap...  277 us
    pallas_call x4, Pallas kernels, update(): pl.pallas_call(functools.partial(kernel, rate), grid=grid, in_specs=[spec...  79 us

profile of v1, /device:TPU:0, one launch (start us, length us, event | category | flops | bytes accessed | tf_op | source)
XLA Modules:
  0.0 363.3 jit_solution(17441489306858459030)
XLA Ops:
  0.7 0.7 convert_element_type.21
  1.3 0.7 convert_element_type.20
  2.0 0.6 pad_maximum_fusion.small_h
  2.7 277.1 %block_kernel.1 = (bf16[256,1024]{1,0:T(8,128)(2,1)}, bf16[256,1024]{1,0:T(8,128)(2,1)}, bf16[4,2048,1152]{2,1,0:T(8,128)(2,1)}, f32[8,1024]{1,0:T(8,128)}) custom-call(bf16[256,1024]{1,0:T(8,128)(2,1)} %bitcast.6, bf16[256,1024]{1,0:T(8,128)(2,1)} %bitcast.7, bf16[512,3072]{1,0:T(8,128)(2,1)} %w.4, bf16[512,1024]{1,0:T(8,128)(2,1)} %w.5, ...), custom_call_target="tpu_custom_call" | custom-call | flops 56371445760 | bytes 62914560 | tf_op jit(solution)/shard_map/block_kernel/pallas_call | solution.py:778
  279.8 15.4 %update_in.1 = (f32[512,3072]{1,0:T(8,128)}, f32[512,3072]{1,0:T(8,128)}, f32[512,3072]{1,0:T(8,128)}) custom-call(bf16[512,3072]{1,0:T(8,128)(2,1)} %w.4, bf16[512,3072]{1,0:T(8,128)(2,1)} %m.4, bf16[512,3072]{1,0:T(8,128)(2,1)} %v.4, bf16[4,2048,1152]{2,1,0:T(8,128)(2,1)} %get-tuple-element.38.g), custom_call_target="tpu_custom_call" | custom-call | flops 18874368 | bytes 31457280 | tf_op jit(solution)/shard_map/update_in/pallas_call | solution.py:851
  295.2 6.1 %update_out.1 = (f32[512,1024]{1,0:T(8,128)}, f32[512,1024]{1,0:T(8,128)}, f32[512,1024]{1,0:T(8,128)}) custom-call(bf16[512,1024]{1,0:T(8,128)(2,1)} %w.5, bf16[512,1024]{1,0:T(8,128)(2,1)} %m.5, bf16[512,1024]{1,0:T(8,128)(2,1)} %v.5, bf16[4,2048,1152]{2,1,0:T(8,128)(2,1)} %get-tuple-element.38.g), custom_call_target="tpu_custom_call" | custom-call | flops 6291456 | bytes 10485760 | tf_op jit(solution)/shard_map/update_out/pallas_call | solution.py:851
  301.3 37.9 %update_gate.1 = (f32[2,512,4608]{2,1,0:T(8,128)}, f32[2,512,4608]{2,1,0:T(8,128)}, f32[2,512,4608]{2,1,0:T(8,128)}) custom-call(bf16[2,512,4608]{2,1,0:T(8,128)(2,1)} %w.6, bf16[2,512,4608]{2,1,0:T(8,128)(2,1)} %m.6, bf16[2,512,4608]{2,1,0:T(8,128)(2,1)} %v.6, bf16[4,2048,1152]{2,1,0:T(8,128)(2,1)} %get-tuple-element.38.g), custom_call_target="tpu_custom_call" | custom-call | flops 56623104 | bytes 94371840 | tf_op jit(solution)/shard_map/update_gate/pallas_call | solution.py:851
  339.2 0.0 copy-start.2
  339.2 0.0 copy-start.4
  339.2 0.0 copy-start.5
  339.3 0.0 copy-start.3
  339.3 0.0 copy-start.6
  339.3 0.0 copy-start.7
  339.3 0.0 copy-start.1
  339.3 0.0 copy-start
  339.3 19.6 %update_down.1 = (f32[4608,512]{1,0:T(8,128)}, f32[4608,512]{1,0:T(8,128)}, f32[4608,512]{1,0:T(8,128)}) custom-call(bf16[4608,512]{1,0:T(8,128)(2,1)} %w.7, bf16[4608,512]{1,0:T(8,128)(2,1)} %m.7, bf16[4608,512]{1,0:T(8,128)(2,1)} %v.7, bf16[4,2048,1152]{2,1,0:T(8,128)(2,1)} %get-tuple-element.38.g), custom_call_target="tpu_custom_call" | custom-call | flops 28311552 | bytes 47185920 | tf_op jit(solution)/shard_map/update_down/pallas_call | solution.py:851
  358.9 0.0 copy-done.2
  358.9 0.0 copy-done.4
  358.9 0.0 copy-done.5
  358.9 1.4 multiply_subtract_fusion
  360.3 0.0 copy-done.3
  360.3 0.0 copy-done.6
  360.3 0.0 copy-done.7
  360.3 1.4 multiply_subtract_fusion.1
  361.7 0.0 copy-done.1
  361.7 0.8 copy.42
  362.5 0.0 copy-done
  362.5 0.8 copy.43
  (1 shorter events, 0.0 us)
Async XLA Ops:
  339.2 19.7 %copy-start.2 = (bf16[3,512]{1,0:T(4,128)(2,1)S(1)}, bf16[3,512]{1,0:T(4,128)(2,1)}, u32[]{:S(2)}) copy-start(bf16[3,512]{1,0:T(4,128)(2,1)} %param.34) | copy-start | bytes 9220
  339.2 19.7 %copy-start.4 = (bf16[3,512]{1,0:T(4,128)(2,1)S(1)}, bf16[3,512]{1,0:T(4,128)(2,1)}, u32[]{:S(2)}) copy-start(bf16[3,512]{1,0:T(4,128)(2,1)} %param.35) | copy-start | bytes 9220
  339.2 19.7 %copy-start.5 = (bf16[3,512]{1,0:T(4,128)(2,1)S(1)}, bf16[3,512]{1,0:T(4,128)(2,1)}, u32[]{:S(2)}) copy-start(bf16[3,512]{1,0:T(4,128)(2,1)} %param.36) | copy-start | bytes 9220
  339.3 21.0 %copy-start.3 = (bf16[2,512]{1,0:T(2,128)(2,1)S(1)}, bf16[2,512]{1,0:T(2,128)(2,1)}, u32[]{:S(2)}) copy-start(bf16[2,512]{1,0:T(2,128)(2,1)} %param.37) | copy-start | bytes 6148
  339.3 21.0 %copy-start.6 = (bf16[2,512]{1,0:T(2,128)(2,1)S(1)}, bf16[2,512]{1,0:T(2,128)(2,1)}, u32[]{:S(2)}) copy-start(bf16[2,512]{1,0:T(2,128)(2,1)} %param.38) | copy-start | bytes 6148
  339.3 21.0 %copy-start.7 = (bf16[2,512]{1,0:T(2,128)(2,1)S(1)}, bf16[2,512]{1,0:T(2,128)(2,1)}, u32[]{:S(2)}) copy-start(bf16[2,512]{1,0:T(2,128)(2,1)} %param.39) | copy-start | bytes 6148
  339.3 22.4 %copy-start.1 = (bf16[256,1024]{1,0:T(8,128)(2,1)S(1)}, bf16[256,1024]{1,0:T(8,128)(2,1)}, u32[]{:S(2)}) copy-start(bf16[256,1024]{1,0:T(8,128)(2,1)} %get-tuple-element.36) | copy-start | bytes 1572868
  339.3 23.2 %copy-start = (bf16[256,1024]{1,0:T(8,128)(2,1)S(1)}, bf16[256,1024]{1,0:T(8,128)(2,1)}, u32[]{:S(2)}) copy-start(bf16[256,1024]{1,0:T(8,128)(2,1)} %get-tuple-element.37) | copy-start | bytes 1572868

commit v2 on v1

v2 whole, which is shorter than its diff:
```python
import functools

import jax
import jax.numpy as jnp
from jax import lax
from jax.experimental import pallas as pl
from jax.experimental.pallas import tpu as pltpu
from jax.sharding import PartitionSpec as P

STEP = 10
norm_eps = 1e-05
beta_one = 0.9
beta_two = 0.95
adam_eps = 1e-08
decay_rate = 0.1
small_rate = 0.4

BF = jnp.bfloat16
F32 = jnp.float32
MESH = pl.DeviceIdType.MESH
GROUPS = 3
CHUNK = 128
TILE = 16
PLAN = (
    (0, 0, 0, 0, 1),
    (0, 0, 0, 0, 2),
    (0, 0, 0, 1, 3),
    (0, 0, 1, 3, 5),
    (0, 0, 2, 4, 6),
    (0, 1, 3, 5, 8),
    (0, 2, 4, 6, 10),
    (0, 4, 6, 8, 11),
    (0, 10, 13, 16, 20),
    (4, 13, 16, 18, 23),
    (8, 15, 18, 20, 25),
    (13, 19, 22, 24, 28),
    (17, 23, 26, 28, 31),
)
HELD = 40

SLOTS = 64
SPOTS = 16


def dot(a, b):
    return lax.dot_general(a, b, (((1,), (0,)), ((), ())), preferred_element_type=F32)


def dot_nt(a, b):
    return lax.dot_general(a, b, (((1,), (1,)), ((), ())), preferred_element_type=F32)


def dot_tn(a, b):
    return lax.dot_general(a, b, (((0,), (0,)), ((), ())), preferred_element_type=F32)


def block_kernel(
    dims,
    tok_h, cot_h, in_h, out_h, gu_h, dn_h, small_h,
    block_out, token_grad, grads, mine, other, small_grads,
    WG, WD, WIN, WOUT, SM, TOK, N1, N2, CT, ML,
    PROJ, MX, CONV, GATED, GCO, ACT, HID, FA, FB, GS, GO, RX,
    MID, GM, P32, SC, RC, SY, RY, SG,
    ss, rs, ls, xs, xr, z1s, z1r, z2s, z2r, ts, tr, ys, yr, c1s, c1r, c2s, c2r, gl,
    ready_w, ready_a,
):
    D, T, FQ, F = dims
    H, Q, R, FG = D // 2, FQ // 2, 4 * T, F // GROUPS
    MT = H // 2
    GR = H + H // 2
    NCH = 2 * (GROUPS + 1) * GR // CHUNK
    PER = 2 * GR // CHUNK
    NGU = 2 * H // CHUNK
    z = lax.axis_index("rep")
    s = lax.axis_index("seq")
    x = lax.axis_index("shard")
    y, c = s // 2, s % 2
    h = z % 2
    is_mid = jnp.logical_and(z > 0, z < 3)
    is_end = jnp.logical_or(z == 0, z == 3)
    xo = 1 - x
    xp = (z, s, xo)
    cp = (z, 2 * y + 1 - c, x)
    yp = (z, 2 * (1 - y) + c, x)
    zp = (z + 1 - 2 * h, s, x)
    mp = (3 - z, s, x)

    def block(i):
        return 2 * (y + (i // 2) * (1 - 2 * y)) + c + (i % 2) * (1 - 2 * c)

    def at(start, size, unit):
        return pl.ds(pl.multiple_of(start, unit), size)

    def rows(m, n=T):
        return at(m * n, n, n)

    slots, spots = {}, {}

    def remote(name, src, dst, dev):
        k = slots.setdefault(name, len(slots))
        return pltpu.make_async_remote_copy(
            src_ref=src, dst_ref=dst, send_sem=ss.at[k], recv_sem=rs.at[k], device_id=dev, device_id_type=MESH
        )

    def local(name, src, dst):
        return pltpu.make_async_copy(src, dst, ls.at[spots.setdefault(name, len(spots))])

    barrier = pltpu.get_barrier_semaphore()
    for dev in (xp, cp, yp, zp):
        pl.semaphore_signal(barrier, inc=1, device_id=dev, device_id_type=MESH)

    @pl.when(is_mid)
    def _():
        pl.semaphore_signal(barrier, inc=1, device_id=mp, device_id_type=MESH)

    def weight(name, owner, half=None):
        kind, p = name.split("_")
        p = int(p)
        if half is None:
            half, parts = 0, 1
        else:
            parts = 2
        n = H // parts
        if kind == "in":
            return WIN.at[at(H * owner + n * half, n, n), FQ * p : FQ * (p + 1)]
        if kind == "out":
            n = Q // parts
            return WOUT.at[at(Q * owner + n * half, n, n)]
        if kind == "down":
            n = FG // parts
            return WD.at[at(FG * p + n * half, n, n), at(H * owner, H, H)]
        j = 0 if kind == "gate" else 1
        return WG.at[at(GR + D * p + H * owner + n * half, n, H // 2), FG * j : FG * (j + 1)]

    def weight_source(name, half=None):
        kind, p = name.split("_")
        p = int(p)
        parts = 1 if half is None else 2
        first = 0 if half is None else half
        n = H // parts
        if kind == "in":
            dst = at(H * x + n * first, n, n)
            return [
                (in_h.at[at(n * first, n, n), at(D * p + H * k + Q * s, Q, Q)], WIN.at[dst, pl.ds(FQ * p + Q * k, Q)])
                for k in range(2)
            ]
        dst = weight(name, x, half)
        if kind == "out":
            n = Q // parts
            return [(out_h.at[at(Q * s + n * first, n, n)], dst)]
        if kind == "down":
            n = FG // parts
            return [(dn_h.at[at(F * s + FG * p + n * first, n, n)], dst)]
        j = 0 if kind == "gate" else 1
        return [(gu_h.at[j, at(n * first, n, n), at(F * s + FG * p, FG, FG)], dst)]

    loads = [
        local("tok", tok_h, TOK),
        local("small", small_h, SM.at[x]),
        local("ct", cot_h, CT.at[rows(s)]),
    ]
    order = ["in_0", "in_1", "in_2", "out_0"]
    for g in range(GROUPS):
        order += ["gate_%d" % g, "up_%d" % g, "down_%d" % g]
    for name in order:
        for src, dst in weight_source(name):
            loads.append(local("in" if name[:3] == "in_" else name.replace("out_0", "out"), src, dst))
    for copy in loads:
        copy.start()

    def local_wait(name):
        if name == "tok":
            copy = local(name, tok_h, TOK)
        elif name == "small":
            copy = local(name, small_h, SM.at[x])
        elif name == "ct":
            copy = local(name, cot_h, CT.at[rows(s)])
        elif name == "in":
            copy = local(name, WIN.at[rows(x, H)], WIN.at[rows(x, H)])
        else:
            here = weight(name if name != "out" else "out_0", x)
            copy = local(name, here, here)
        copy.wait()

    @pl.when(is_mid)
    def _():
        pl.semaphore_wait(barrier, 5)

    @pl.when(is_end)
    def _():
        pl.semaphore_wait(barrier, 4)

    def weight_pass(name):
        here = weight(name, xo, h)
        remote(name, here, here, xp).wait_recv()
        remote(name + "_z", here, here, zp).start()

    def weight_wait(name):
        there = weight(name, xo, 1 - h)
        remote(name + "_z", there, there, zp).wait_recv()

    def weight_passed(name):
        here = weight(name, xo, h)
        remote(name + "_z", here, here, zp).wait_send()

    def group_wait(g):
        for kind in ("gate_", "up_", "down_"):
            local_wait(kind + str(g))
            weight_wait(kind + str(g))

    def gather_copy(name, buf, kind, src=None):
        m = block(2) if kind == "f" else s
        return remote(
            name + "_" + kind, buf.at[rows(m)] if src is None else src, buf.at[rows(m)], yp if kind == "y" else cp
        )

    def gather_start(name, buf):
        gather_copy(name, buf, "y").start()
        gather_copy(name, buf, "c").start()

    def gather_step(name, buf, i, between=None):
        @pl.when(i == 1)
        def _():
            remote(name + "_c", buf.at[rows(block(1))], buf.at[rows(block(1))], cp).wait_recv()

        @pl.when(i == 2)
        def _():
            remote(name + "_y", buf.at[rows(block(2))], buf.at[rows(block(2))], yp).wait_recv()
            if between is not None:
                between()
            gather_copy(name, buf, "f").start()

        @pl.when(i == 3)
        def _():
            remote(name + "_f", buf.at[rows(block(3))], buf.at[rows(block(3))], cp).wait_recv()

    remote("small", small_h, SM.at[x], xp).start()
    gather_copy("n1", N1, "y", tok_h).start()
    gather_copy("ct", CT, "y", cot_h).start()
    gather_copy("ct", CT, "c", cot_h).start()
    for name in order:
        for src, dst in weight_source(name, h):
            remote(name, src, dst, xp).start()

    def sum_core(name, lot, k):
        return remote(name + "_" + str(k), SC.at[lot, k], RC.at[lot, k], cp)

    def sum_y(name, lot):
        return remote(name + "_y", SY.at[lot], RY.at[lot], yp)

    def sum_emit(name, lot, i, partial):
        @pl.when(i % 2 == 0)
        def _():
            P32[i // 2] = partial

        @pl.when(i == 1)
        def _():
            SC[lot, 1] = partial.astype(BF)
            sum_core(name, lot, 1).start()

        @pl.when(i == 3)
        def _():
            SC[lot, 0] = partial.astype(BF)
            sum_core(name, lot, 0).start()

    def sum_cross(name, lot):
        sum_core(name, lot, 0).wait_recv()

        def add(r):
            SY[lot, r] = (P32[1, r] + RC[lot, 0, r].astype(F32)).astype(BF)

        tiles(T, add, 32)
        sum_y(name, lot).start()

    def sum_wait(name, lot):
        sum_core(name, lot, 1).wait_recv()
        sum_y(name, lot).wait_recv()

    def sum_rows(lot, r):
        return P32[0, r] + RC[lot, 1, r].astype(F32) + RY[lot, r].astype(F32)

    def sum_done(name, lot):
        sum_core(name, lot, 0).wait_send()
        sum_core(name, lot, 1).wait_send()
        sum_y(name, lot).wait_send()

    def tiles(n, body, size=TILE):
        def step(t, carry):
            body(pl.ds(pl.multiple_of(t * size, size), size))
            return carry

        lax.fori_loop(0, n // size, step, 0)

    def blocks(body, order=(0, 1, 2, 3)):
        first, step = order[0], order[1] - order[0]

        def turn(t, carry):
            i = first + step * t
            body(i, block(i))
            return carry

        lax.fori_loop(0, len(order), turn, 0)

    def gain(k):
        return jnp.concatenate([SM[0, 3 + k : 4 + k, :], SM[1, 3 + k : 4 + k, :]], axis=1)

    def tap(k):
        cols = rows(s, Q)
        return jnp.concatenate([SM[0, k : k + 1, cols], SM[1, k : k + 1, cols]], axis=1)

    local_wait("tok")
    local_wait("small")
    remote("small", small_h, SM.at[xo], xp).wait()
    SG[0] = jnp.zeros_like(SG[0])
    MX[0:8] = jnp.zeros((8, FQ), F32)
    GCO[R : R + 8] = jnp.zeros((8, FQ), F32)
    gain_one = gain(0)

    def norm_one(src, first, m):
        def one(r):
            v = src[at(first + r.start, 32, 32)].astype(F32)
            scale = lax.rsqrt(jnp.mean(v * v, axis=-1, keepdims=True) + norm_eps)
            N1[at(m * T + r.start, 32, 32)] = (v * scale * gain_one).astype(BF)

        tiles(T, one, 32)

    norm_one(TOK, 0, s)
    gather_copy("n1", N1, "c").start()

    for name in order[:3]:
        weight_pass(name)
    local_wait("in")
    for name in order[:3]:
        weight_wait(name)
    weight_pass("out_0")

    def project(i, m):
        gather_step("n1", N1, i, lambda: norm_one(N1, block(2) * T, block(2)))
        p = dot(N1[rows(m)], WIN[...])
        PROJ[rows(m)] = p
        mixed = (p[:, :FQ] * p[:, 2 * FQ :]).astype(BF)
        MX[at(8 + m * T, T, 8)] = mixed.astype(F32)

    blocks(project)
    weight_pass("gate_0")
    local_wait("out")
    weight_wait("out_0")

    def convolve(i, m):
        ext = MX[at(m * T, T + 8, 8)]
        conv = tap(0) * ext[6 : 6 + T] + tap(1) * ext[7 : 7 + T] + tap(2) * ext[8 : 8 + T]
        CONV[rows(m)] = conv
        gated = (PROJ[rows(m), FQ : 2 * FQ] * conv).astype(BF)
        GATED[rows(m)] = gated
        sum_emit("ro", 0, i, dot(gated, WOUT[...]))

    blocks(convolve, (3, 2))
    weight_pass("up_0")
    sum_cross("ro", 0)
    blocks(convolve, (1, 0))
    for name in ("down_0", "gate_1", "up_1"):
        weight_pass(name)
    sum_wait("ro", 0)

    gain_two = gain(1)

    def norm_two(r):
        v = TOK[r].astype(F32) + sum_rows(0, r)
        MID[r] = v
        scale = lax.rsqrt(jnp.mean(v * v, axis=-1, keepdims=True) + norm_eps)
        N2[at(s * T + r.start, 32, 32)] = (v * scale * gain_two).astype(BF)

    tiles(T, norm_two, 32)
    gather_start("n2", N2)
    sum_done("ro", 0)
    weight_pass("down_1")

    def feed(g):
        def unit(i, m):
            if g == 0:
                gather_step("n2", N2, i)
                gather_step("ct", CT, i)
            FA[...] = dot(N2[rows(m)], WG[GR + D * g : GR + D * (g + 1)])
            FB[...] = dot_nt(CT[rows(m)], WD[FG * g : FG * (g + 1)])

            def act(r):
                gate, up, gh = FA[r, 0:FG], FA[r, FG:], FB[r]
                sig = jax.nn.sigmoid(gate)
                silu = gate * sig
                ro = at(GR + R * g + m * T + r.start, 32, 32)
                ACT[ro, 0:FG] = (gh * up * sig * (1.0 + gate * (1.0 - sig))).astype(BF)
                ACT[ro, FG:] = (gh * silu).astype(BF)
                HID[at(m * T + r.start, 32, 32), FG * g : FG * (g + 1)] = (silu * up).astype(BF)

            tiles(T, act, 32)

        return unit

    def group_grad(g, dst, owner):
        base = GR * g

        def step(t, carry):
            lhs = N2[:, at(H * owner + MT * t, MT, MT)]
            dst[at(base + MT * t, MT, MT)] = dot_tn(lhs, ACT[GR + R * g : GR + R * (g + 1)]).astype(BF)
            lhs = CT[:, at(H * owner + MT * t, MT, MT)]
            low = dot_tn(lhs, HID[:, FG * g : FG * (g + 1)]).astype(BF)
            for j in range(2):
                dst[at(base + H + CHUNK * t, CHUNK, CHUNK), FG * j : FG * (j + 1)] = low[CHUNK * j : CHUNK * (j + 1)]
            return carry

        lax.fori_loop(0, H // MT, step, 0)

    def chunk(ref, k):
        return ref.at[rows(k // 2, CHUNK), at(FG * (k % 2), FG, FG)]

    def step_copy(src, dst, send, recv, k, dev):
        return pltpu.make_async_remote_copy(
            src_ref=src, dst_ref=dst, send_sem=send.at[k], recv_sem=recv.at[k], device_id=dev, device_id_type=MESH
        )

    def x_copy(k):
        return step_copy(chunk(GS, k), chunk(RX, k), xs, xr, k, xp)

    def z1_copy(k):
        return step_copy(chunk(GO, k), chunk(WG, k), z1s, z1r, k, zp)

    def z2_copy(k):
        return step_copy(chunk(RX, k), chunk(ACT, k), z2s, z2r, k, mp)

    def t_copy(k):
        return step_copy(chunk(GO, k), chunk(WG, k), ts, tr, k, zp)

    def is_wide(k):
        return jnp.logical_and(k < GROUPS * PER, k % PER < NGU)

    def wide_at(k, m):
        return grads.at[m, rows((NGU // 2) * (k // PER) + (k % PER) // 2, CHUNK), at(FG * (k % 2), FG, FG)]

    def late_at(k, ref, inner):
        if inner:
            row = ((PER - NGU) // 2) * GROUPS + (k - GROUPS * PER) // 2
        else:
            row = ((PER - NGU) // 2) * (k // PER) + (k % PER - NGU) // 2
        return ref.at[rows(row, CHUNK), at(FG * (k % 2), FG, FG)]

    def y_copy(k, src):
        return step_copy(chunk(src, k), wide_at(k, s), ys, yr, k, yp)

    def c2_copy(k):
        m = block(2)
        return step_copy(wide_at(k, m), wide_at(k, m), c2s, c2r, k, cp)

    def spread(k, src):
        @pl.when(is_wide(k))
        def _():
            y_copy(k, src).start()
            step_copy(chunk(src, k), wide_at(k, s), c1s, c1r, k, cp).start()
            pltpu.make_async_copy(chunk(src, k), wide_at(k, s), gl.at[k]).start()

        for inner in (False, True):
            if inner:
                cond = k >= GROUPS * PER
            else:
                cond = jnp.logical_and(k < GROUPS * PER, k % PER >= NGU)

            @pl.when(cond)
            def _():
                step_copy(chunk(src, k), late_at(k, other, inner), c1s, c1r, k, cp).start()
                pltpu.make_async_copy(chunk(src, k), late_at(k, mine, inner), gl.at[k]).start()

    def add(k, dst, one, two):
        total = chunk(one, k)[...].astype(F32) + chunk(two, k)[...].astype(F32)
        chunk(dst, k)[...] = total.astype(BF)

    def add_x(k):
        x_copy(k).wait_recv()
        add(k, GO, GO, RX)
        pl.when(is_end)(lambda: z1_copy(k).start())

    def add_end(k):
        @pl.when(is_mid)
        def _():
            z1_copy(k).wait_recv()
            add(k, RX, GO, WG)
            z2_copy(k).start()

    def add_mid(k):
        @pl.when(is_mid)
        def _():
            z2_copy(k).wait_recv()
            add(k, GO, RX, ACT)
            t_copy(k).start()
            spread(k, GO)

    def take(k):
        @pl.when(is_end)
        def _():
            t_copy(k).wait_recv()
            spread(k, WG)

    def hand(k):
        @pl.when(is_wide(k))
        def _():
            m = block(2)
            step_copy(wide_at(k, m), wide_at(k, m), ys, yr, k, yp).wait_recv()
            c2_copy(k).start()

    stages = (hand, take, add_mid, add_end, add_x)
    place = [0] * len(stages)

    def advance(*goals, late=True):
        first = tuple(place)
        n = max(goal - at for goal, at in zip(goals, first))

        def step(t, carry):
            for body, at, goal in zip(stages, first, goals):
                if goal > at:
                    skip = n - (goal - at) if late else 0
                    pl.when(jnp.logical_and(t >= skip, t < skip + goal - at))(functools.partial(body, at + t - skip))
            return carry

        lax.fori_loop(0, n, step, 0)
        place[:] = goals

    def send(first, last):
        def step(k, carry):
            x_copy(k).start()
            return carry

        lax.fori_loop(first, last, step, 0)

    local_wait("ct")
    group_wait(0)
    blocks(feed(0), (0, 1))
    weight_pass("gate_2")
    group_wait(1)
    weight_pass("up_2")
    blocks(feed(1), (0, 1))
    blocks(feed(0), (2, 3))
    group_grad(0, GS, xo)
    send(0, PER)
    weight_pass("down_2")
    group_grad(0, GO, x)
    advance(*PLAN[0])
    blocks(feed(1), (2, 3))
    advance(*PLAN[1])
    group_grad(1, GS, xo)
    send(PER, 2 * PER)
    advance(*PLAN[2])
    group_wait(2)
    blocks(feed(2), (0, 1, 2, 3))
    advance(*PLAN[3])
    group_grad(2, GS, xo)
    send(2 * PER, 3 * PER)
    advance(*PLAN[4])

    def back_feed(i, m):
        partial = dot_nt(ACT[at(GR + m * T, T, T)], WG[GR : GR + D])
        for g in range(1, GROUPS):
            partial = partial + dot_nt(ACT[at(GR + R * g + m * T, T, T)], WG[GR + D * g : GR + D * (g + 1)])
        sum_emit("rg", 1, i, partial)

    blocks(back_feed, (3, 2))
    sum_cross("rg", 1)
    advance(*PLAN[5])
    blocks(back_feed, (1, 0))
    for g in range(GROUPS):
        weight_passed("gate_%d" % g)
        weight_passed("up_%d" % g)
    pl.semaphore_signal(ready_w, inc=1, device_id=zp, device_id_type=MESH)
    group_grad(1, GO, x)
    advance(*PLAN[6])
    group_grad(2, GO, x)

    @pl.when(is_mid)
    def _():
        pl.semaphore_signal(ready_a, inc=1, device_id=mp, device_id_type=MESH)

    pl.semaphore_wait(ready_w, 1)

    @pl.when(is_mid)
    def _():
        pl.semaphore_wait(ready_a, 1)

    advance(*PLAN[7])

    sum_wait("rg", 1)

    def back_two(t, acc):
        r = at(t * TILE, TILE, TILE)
        v = MID[r]
        scale = lax.rsqrt(jnp.mean(v * v, axis=-1, keepdims=True) + norm_eps)
        unit = v * scale
        e = sum_rows(1, r)
        eu = e * unit
        ew = e * gain_two
        grad = scale * (ew - unit * jnp.mean(ew * unit, axis=-1, keepdims=True))
        ro = at(s * T + t * TILE, TILE, TILE)
        gm = CT[ro].astype(F32) + grad
        GM[r] = gm
        ML[ro] = gm.astype(BF)
        return acc + jnp.sum(eu, axis=0, keepdims=True)

    SG[0, 4:5, :] = lax.fori_loop(0, T // TILE, back_two, jnp.zeros((1, D), F32))
    gather_start("ml", ML)
    sum_done("rg", 1)
    advance(*PLAN[8])

    def gated_back(i, m):
        gather_step("ml", ML, i)
        gg = dot_nt(ML[rows(m)], WOUT[...])
        gco = gg * PROJ[rows(m), FQ : 2 * FQ]
        GCO[rows(m)] = gco
        PROJ[rows(m), FQ : 2 * FQ] = gg * CONV[rows(m)]

    blocks(gated_back)
    for kind in "cyf":
        gather_copy("n2", N2, kind).wait_send()

    def conv_back(t, acc):
        i = 3 - t
        m = block(i)
        gco = GCO[at(m * T, T + 8, 8)]
        ext = MX[at(m * T, T + 8, 8)]
        here = gco[0:T]
        gm = tap(2) * here + tap(1) * gco[1 : 1 + T] + tap(0) * gco[2 : 2 + T]
        p = PROJ[rows(m)]
        low = jnp.concatenate([gm * p[:, 2 * FQ :], p[:, FQ : 2 * FQ], gm * p[:, :FQ]], axis=1).astype(BF)
        N2[rows(m), 0 : 3 * FQ] = low
        sum_emit("ri", 1, i, dot_nt(low, WIN[...]))
        return tuple(
            a + jnp.sum(here * ext[6 + k : 6 + k + T], axis=0, keepdims=True) for k, a in enumerate(acc)
        )

    conv_grads = lax.fori_loop(0, 4, conv_back, (jnp.zeros((1, FQ), F32),) * 3)
    for k in range(3):
        SG[0, k : k + 1, rows(s, Q)] = conv_grads[k][:, :Q]
        SG[0, k : k + 1, at(H + s * Q, Q, Q)] = conv_grads[k][:, Q:]
    sum_cross("ri", 1)

    def io_grad(dst, owner):
        base = GROUPS * GR

        def step(t, carry):
            lhs = N1[:, at(H * owner + MT * t, MT, MT)]
            dst[at(base + MT * t, MT, MT)] = dot_tn(lhs, N2[:, 0 : 3 * FQ]).astype(BF)
            right = GATED[:, rows(owner, Q)]
            for j in range(2):
                lhs = ML[:, at(H * j + MT * t, MT, MT)]
                low = dot_tn(lhs, right).astype(BF)
                for k in range(2):
                    dst[at(base + H + CHUNK * t, CHUNK, CHUNK), FG * k + Q * j : FG * k + Q * (j + 1)] = low[
                        CHUNK * k : CHUNK * (k + 1)
                    ]
            for k in range(2):
                dst[at(base + H + CHUNK * t, CHUNK, CHUNK), FG * k + 2 * Q : FG * (k + 1)] = jnp.zeros(
                    (CHUNK, FG - 2 * Q), BF
                )
            return carry

        lax.fori_loop(0, H // MT, step, 0)

    io_grad(GS, xo)
    send(GROUPS * PER, HELD)
    advance(*PLAN[9])
    io_grad(GO, x)
    advance(*PLAN[10])

    sum_wait("ri", 1)
    low_out = SC.at[0, 0]

    def back_one(t, acc):
        r = at(t * TILE, TILE, TILE)
        v = TOK[r].astype(F32)
        scale = lax.rsqrt(jnp.mean(v * v, axis=-1, keepdims=True) + norm_eps)
        unit = v * scale
        e = sum_rows(1, r)
        eu = e * unit
        ew = e * gain_one
        grad = scale * (ew - unit * jnp.mean(ew * unit, axis=-1, keepdims=True))
        low_out[r] = (GM[r] + grad).astype(BF)
        return acc + jnp.sum(eu, axis=0, keepdims=True)

    SG[0, 3:4, :] = lax.fori_loop(0, T // TILE, back_one, jnp.zeros((1, D), F32))
    out_copy = pltpu.make_async_copy(low_out, token_grad, ls.at[spots["tok"]])
    out_copy.start()
    sum_done("ri", 1)

    def small_start(name, dev, k):
        remote(name, SG.at[0], SG.at[k], dev).start()

    def small_end(name, dev, k):
        remote(name, SG.at[0], SG.at[k], dev).wait()
        SG[0] = SG[0] + SG[k]

    small_start("sg_c", cp, 2)
    advance(*PLAN[11])
    small_end("sg_c", cp, 2)
    small_start("sg_y", yp, 3)
    out_copy.wait()

    def down(i, m):
        sum_emit("rr", 0, i, dot(HID[rows(m)], WD[...]))

    blocks(down, (3, 2, 1, 0))
    sum_cross("rr", 0)
    small_end("sg_y", yp, 3)
    small_start("sg_x", xp, 1)
    send(HELD, NCH)
    advance(*PLAN[12])

    def on(first, last):
        for k in range(first, last + 1, 2):
            advance(*(min(max(k - lag, at), NCH) for lag, at in zip((12, 9, 6, 3, 0), place)))

    on(32, 38)
    sum_wait("rr", 0)
    sum_done("rr", 0)

    def result(r):
        low_out[r] = (MID[r] + sum_rows(0, r)).astype(BF)

    tiles(T, result, 32)
    out_copy = pltpu.make_async_copy(low_out, block_out, ls.at[spots["tok"]])
    out_copy.start()
    on(40, 42)
    small_end("sg_x", xp, 1)
    pl.when(is_end)(lambda: small_start("sg_a", zp, 4))
    on(44, 46)

    @pl.when(is_end)
    def _():
        remote("sg_a", SG.at[0], SG.at[4], zp).wait_send()

    @pl.when(is_mid)
    def _():
        remote("sg_a", SG.at[0], SG.at[4], zp).wait_recv()
        SG[0] = SG[0] + SG[4]
        small_start("sg_b", mp, 5)

    on(48, 48)

    @pl.when(is_mid)
    def _():
        remote("sg_b", SG.at[0], SG.at[5], mp).wait()
        SG[6] = SG[0] + SG[5]
        remote("sg_t", SG.at[6], SG.at[6], zp).start()

    advance(*(NCH,) * 5, late=False)

    @pl.when(is_mid)
    def _():
        remote("sg_t", SG.at[6], SG.at[6], zp).wait_send()

    @pl.when(is_end)
    def _():
        remote("sg_t", SG.at[6], SG.at[6], zp).wait_recv()

    small_copy = pltpu.make_async_copy(SG.at[6], small_grads, ls.at[spots["small"]])
    small_copy.start()

    def finish(k, carry):
        x_copy(k).wait_send()

        @pl.when(is_end)
        def _():
            z1_copy(k).wait_send()

        @pl.when(is_mid)
        def _():
            z2_copy(k).wait_send()
            t_copy(k).wait_send()

        @pl.when(is_wide(k))
        def _():
            y_copy(k, GO).wait_send()
            c2_copy(k).wait()

        here = chunk(GO, k)
        step_copy(here, here, c1s, c1r, k, cp).wait()
        pltpu.make_async_copy(here, here, gl.at[k]).wait()
        return carry

    lax.fori_loop(0, NCH, finish, 0)
    out_copy.wait()
    small_copy.wait()
    for name in order:
        here = weight(name, x, h)
        remote(name, here, here, xp).wait_send()
        if name[0] not in "gu":
            weight_passed(name)
    for name, buf in (("n1", N1), ("ct", CT), ("ml", ML)):
        for kind in "cyf":
            gather_copy(name, buf, kind).wait_send()


def run_block(tokens, cotangent, in_proj, out_proj, gate_up, down_proj, small):
    T, D = tokens.shape
    F = gate_up.shape[2] // 4
    FQ = D // 4
    R = 4 * T
    H = D // 2
    W2 = 2 * F // GROUPS
    GR = H + H // 2
    NR = (GROUPS + 1) * GR
    dims = (D, T, FQ, F)
    NCH = 2 * NR // CHUNK
    hbm = pl.BlockSpec(memory_space=pltpu.HBM)
    dma = pltpu.SemaphoreType.DMA
    vmem = pltpu.VMEM
    late = jax.ShapeDtypeStruct((GROUPS * H // 2 + GR, W2), BF)
    scratch = [
        vmem((GR + NR, W2), BF),
        vmem((F, D), BF),
        vmem((D, 3 * FQ), BF),
        vmem((FQ, D), BF),
        vmem((2, 8, H), F32),
        vmem((T, D), BF),
        vmem((R, D), BF),
        vmem((R, D), BF),
        vmem((R, D), BF),
        vmem((R, D), BF),
        vmem((R, 3 * FQ), F32),
        vmem((R + 8, FQ), F32),
        vmem((R, FQ), F32),
        vmem((R, FQ), BF),
        vmem((R + 8, FQ), F32),
        vmem((GR + NR, W2), BF),
        vmem((R, F), BF),
        vmem((T, W2), F32),
        vmem((T, W2 // 2), F32),
        vmem((NR, W2), BF),
        vmem((NR, W2), BF),
        vmem((NR, W2), BF),
        vmem((T, D), F32),
        vmem((T, D), F32),
        vmem((2, T, D), F32),
        vmem((2, 2, T, D), BF),
        vmem((2, 2, T, D), BF),
        vmem((2, T, D), BF),
        vmem((2, T, D), BF),
        vmem((7, 8, D), F32),
        dma((SLOTS,)),
        dma((SLOTS,)),
        dma((SPOTS,)),
    ]
    scratch += [dma((NCH,))] * 15
    scratch += [pltpu.SemaphoreType.REGULAR, pltpu.SemaphoreType.REGULAR]
    flops = 6 * R * D * (3 * F + 4 * FQ) * 2
    return pl.pallas_call(
        functools.partial(block_kernel, dims),
        out_shape=(
            jax.ShapeDtypeStruct((T, D), BF),
            jax.ShapeDtypeStruct((T, D), BF),
            jax.ShapeDtypeStruct((4, GROUPS * H, W2), BF),
            late,
            late,
            jax.ShapeDtypeStruct((8, D), F32),
        ),
        in_specs=[hbm] * 7,
        out_specs=(hbm,) * 6,
        scratch_shapes=scratch,
        compiler_params=pltpu.CompilerParams(
            collective_id=0, has_side_effects=True, vmem_limit_bytes=62 * 2**20
        ),
        cost_estimate=pl.CostEstimate(flops=flops, bytes_accessed=60 * 2**20, transcendentals=R * F),
        name="block_kernel",
    )(tokens, cotangent, in_proj, out_proj, gate_up, down_proj, small)


def adamw(weight, first_moment, second_moment, gradient, step_rate, decay_factor):
    first_new = beta_one * first_moment + (1.0 - beta_one) * gradient
    second_new = beta_two * second_moment + (1.0 - beta_two) * gradient * gradient
    adam_ratio = (
        first_new
        / (1.0 - beta_one**STEP)
        / (jnp.sqrt(second_new / (1.0 - beta_two**STEP)) + adam_eps)
    )
    weight_new = weight - step_rate * (adam_ratio + decay_factor * weight)
    return (weight_new, first_new, second_new)


def update_values(rate, w, m, v, grad):
    w, m, v, grad = (a.astype(F32) for a in (w, m, v, grad))
    first = beta_one * m + (1.0 - beta_one) * grad
    second = beta_two * v + (1.0 - beta_two) * grad * grad
    u = second * (1.0 / (1.0 - beta_two**STEP))
    root = u * lax.rsqrt(u) + adam_eps
    return (1.0 - rate * decay_rate) * w - (rate / (1.0 - beta_one**STEP)) * first / root, first, second


def update_gate(rate, where, w, m, v, *refs):
    grads, new = refs[:GROUPS], refs[GROUPS:]
    FG = w.shape[2] // GROUPS
    for g in range(GROUPS):
        cols = slice(FG * g, FG * (g + 1))
        values = update_values(rate, w[0, :, cols], m[0, :, cols], v[0, :, cols], grads[g][0])
        for ref, value in zip(new, values):
            ref[0, :, cols] = value


def update_down(rate, where, w, m, v, *refs):
    one, two, new = refs[:GROUPS], refs[GROUPS : 2 * GROUPS], refs[-3:]
    FG = w.shape[0] // GROUPS
    first = pl.program_id(0) == 0
    for g in range(GROUPS):
        grad = jnp.where(first, one[g][...], two[g][...]).astype(F32)
        for j in range(2):
            at = (slice(FG * g, FG * (g + 1)), slice(CHUNK * j, CHUNK * (j + 1)))
            values = update_values(rate, w[at], m[at], v[at], grad[:, FG * j : FG * (j + 1)].T)
            for ref, value in zip(new, values):
                ref[at] = value


def pick(where, one, two, far_one, far_two):
    c, y = where[0] == 1, where[1] == 1
    near = jnp.where(c, two, one), jnp.where(c, one, two)
    far = jnp.where(c, far_two, far_one), jnp.where(c, far_one, far_two)
    return (
        jnp.where(y, far[0], near[0]), jnp.where(y, far[1], near[1]),
        jnp.where(y, near[0], far[0]), jnp.where(y, near[1], far[1]),
    )


def update_in(rate, where, w, m, v, *refs):
    grads, new = refs[:4], refs[-3:]
    Q = w.shape[1] // 24
    for j in range(6):
        four = pick(where, *(g[:, Q * j : Q * (j + 1)] for g in grads))
        for k in range(4):
            cols = slice((4 * j + k) * Q, (4 * j + k + 1) * Q)
            values = update_values(rate, w[:, cols], m[:, cols], v[:, cols], four[k])
            for ref, value in zip(new, values):
                ref[:, cols] = value


def update_out(rate, where, w, m, v, *refs):
    grads, new = refs[:4], refs[-3:]
    D = w.shape[1]
    Q = w.shape[0] // 4
    FG = grads[0].shape[1] // 2
    for r in range(4):
        for j in range(2):
            cols = slice(D // 2 * j + CHUNK * r, D // 2 * j + CHUNK * (r + 1))
            part = (slice(CHUNK * (r // 2), CHUNK * (r // 2 + 1)), slice(FG * (r % 2) + Q * j, FG * (r % 2) + Q * (j + 1)))
            four = pick(where, *(g[part] for g in grads))
            for k in range(4):
                at = (slice(Q * k, Q * (k + 1)), cols)
                values = update_values(rate, w[at], m[at], v[at], four[k].astype(F32).T)
                for ref, value in zip(new, values):
                    ref[at] = value


def update(kernel, rate, where, state, grads, before, grid, spec, g_specs, name):
    weight = state[0]
    n = grid[0] * grid[1] * spec.block_shape[-1] * spec.block_shape[-2]
    keep = [] if before is None else [pl.BlockSpec(memory_space=pl.ANY)] * 3
    first = 4 + len(grads)
    return pl.pallas_call(
        functools.partial(kernel, rate),
        grid_spec=pltpu.PrefetchScalarGridSpec(
            num_scalar_prefetch=1,
            grid=grid,
            in_specs=[spec] * 3 + list(g_specs) + keep,
            out_specs=(spec,) * 3,
        ),
        out_shape=(jax.ShapeDtypeStruct(weight.shape, F32),) * 3,
        input_output_aliases={} if before is None else {first + i: i for i in range(3)},
        compiler_params=pltpu.CompilerParams(vmem_limit_bytes=56 * 2**20),
        cost_estimate=pl.CostEstimate(flops=12 * n, bytes_accessed=20 * n, transcendentals=2 * n),
        name=name,
    )(where, *state, *grads, *(before or ()))


def fused_body(
    tokens, cotangent, in_proj, in_moment, in_square, out_proj, out_moment, out_square,
    gate_up, gate_moment, gate_square, down_proj, down_moment, down_square,
    conv_kernel, conv_moment, conv_square, norm_gains, gains_moment, gains_square,
):
    T, D = tokens.shape[1:]
    H, Q = D // 2, D // 8
    F = gate_up.shape[2] // 4
    FF, FG = 4 * F, F // GROUPS
    W2 = 2 * FG
    rate = 2.0 * D ** (-0.5)
    down_rate = 2.0 * FF ** (-0.5)
    small = jnp.concatenate(
        [conv_kernel.astype(F32), norm_gains.astype(F32), jnp.zeros((3, H), F32)], axis=0
    )
    block_out, token_grad, grads, mine, other, small_grads = run_block(
        tokens[0], cotangent[0], in_proj, out_proj, gate_up, down_proj, small
    )
    seq = lax.axis_index("seq")
    y, c = seq // 2, seq % 2
    near = jnp.stack([c, y]).astype(jnp.int32)
    far = jnp.stack([c, 1 - y]).astype(jnp.int32)

    gate_state = (gate_up, gate_moment, gate_square)
    down_state = (down_proj, down_moment, down_square)
    in_state = (in_proj, in_moment, in_square)
    out_state = (out_proj, out_moment, out_square)

    def down_step(where, one, two, before, name):
        spec = pl.BlockSpec((F, 2 * CHUNK), lambda k, q, w: (2 * w[1] + w[0] + k * (1 - 2 * w[0]), q))
        g_specs = [pl.BlockSpec((CHUNK, W2), lambda k, q, w, g=g: (2 * g + q * (1 - k) + k, 0)) for g in range(GROUPS)]
        g_specs += [pl.BlockSpec((CHUNK, W2), lambda k, q, w, g=g: (2 * g + q * k, 0)) for g in range(GROUPS)]
        return update(
            update_down, down_rate, where, down_state, (one,) * GROUPS + (two,) * GROUPS, before, (2, 2), spec, g_specs, name
        )

    across = lax.ppermute(mine, "seq", [(i, (i + 2) % 4) for i in range(4)])
    n = H // 256
    gate = update(
        update_gate, rate, near, gate_state, (grads,) * GROUPS, None,
        (2 * n, 4),
        pl.BlockSpec((1, 256, F), lambda r, k, w: (r // n, r % n, k)),
        [pl.BlockSpec((1, 256, FG), lambda r, k, w, g=g: (k, g * n + r % n, r // n)) for g in range(GROUPS)],
        "update_gate",
    )
    down = down_step(near, mine, other, None, "update_down")
    across, gate, down = lax.optimization_barrier((across, gate, down))
    beyond = lax.ppermute(across, "seq", [(i, i + 1 - 2 * (i % 2)) for i in range(4)])
    four = (mine, other, across, beyond)
    down = down_step(far, across, beyond, down, "update_down_far")
    n = 64
    base = GROUPS * H // 2
    inner = update(
        update_in, rate, near, in_state, four, None, (H // n, 1),
        pl.BlockSpec((n, 3 * D), lambda r, k, w: (r, 0)),
        [pl.BlockSpec((n, W2), lambda r, k, w: (base // n + r, 0))] * 4,
        "update_in",
    )
    base += H
    outer = update(
        update_out, rate, near, out_state, four, None, (1, 1),
        pl.BlockSpec((H, D), lambda r, k, w: (0, 0)),
        [pl.BlockSpec((2 * CHUNK, W2), lambda r, k, w: (base // (2 * CHUNK), 0))] * 4,
        "update_out",
    )
    mine_small = lax.dynamic_slice_in_dim(small_grads, lax.axis_index("shard") * H, H, axis=1)
    conv = adamw(
        conv_kernel.astype(F32), conv_moment.astype(F32), conv_square.astype(F32), mine_small[0:3], small_rate, 0.0
    )
    gains = adamw(
        norm_gains.astype(F32), gains_moment.astype(F32), gains_square.astype(F32), mine_small[3:5], small_rate, 0.0
    )
    return (block_out[None], token_grad[None], *inner, *outer, *gate, *down, *conv, *gains)


def shifted(block, axis, distance):
    devices = range(lax.axis_size(axis))
    route = [(i - distance, i) for i in devices if i - distance in devices]
    return lax.ppermute(block, axis, route)


def norm_forward(values, gain_vector):
    norm_scale = lax.rsqrt(jnp.mean(values * values, axis=-1, keepdims=True) + norm_eps)
    unit_rows = values * norm_scale
    return (unit_rows, norm_scale, (unit_rows * gain_vector).astype(jnp.bfloat16))


def norm_backward(grad_normed, unit_rows, norm_scale, gain_vector):
    gain_grad = jnp.sum(grad_normed * unit_rows, axis=(0, 1))
    grad_unit = grad_normed * gain_vector
    grad_values = norm_scale * (
        grad_unit - unit_rows * jnp.mean(grad_unit * unit_rows, axis=-1, keepdims=True)
    )
    return (gain_grad, grad_values)


def plain_body(
    tokens,
    cotangent,
    in_proj,
    in_moment,
    in_square,
    out_proj,
    out_moment,
    out_square,
    gate_up,
    gate_moment,
    gate_square,
    down_proj,
    down_moment,
    down_square,
    conv_kernel,
    conv_moment,
    conv_square,
    norm_gains,
    gains_moment,
    gains_square,
):
    gathered = (
        lax.all_gather(in_proj, "shard", axis=0, tiled=True),
        lax.all_gather(out_proj, "shard", axis=0, tiled=True),
        lax.all_gather(gate_up, "shard", axis=1, tiled=True),
        lax.all_gather(down_proj, "shard", axis=1, tiled=True),
        lax.all_gather(conv_kernel, "shard", axis=1, tiled=True),
        lax.all_gather(norm_gains, "shard", axis=1, tiled=True),
    )
    full_in, full_out, full_gate, full_down, full_conv, full_gains = gathered
    gains_float = full_gains.astype(jnp.float32)
    conv_float = full_conv.astype(jnp.float32)
    inputs = tokens.astype(jnp.float32)
    model_width = inputs.shape[2]
    rows_count = inputs.shape[1]
    unit_one, scale_one, normed_one = norm_forward(inputs, gains_float[0])
    projected = jnp.einsum("scd,de->sce", normed_one, full_in, preferred_element_type=jnp.float32)
    first_gate = projected[:, :, :model_width]
    second_gate = projected[:, :, model_width : 2 * model_width]
    conv_input = projected[:, :, 2 * model_width :]
    mixed_in = (first_gate * conv_input).astype(jnp.bfloat16)
    before = shifted(mixed_in[:, rows_count - 2 :, :], "seq", 1)
    extended = jnp.concatenate([before, mixed_in], axis=1).astype(jnp.float32)
    convolved = (
        conv_float[0] * extended[:, :-2]
        + conv_float[1] * extended[:, 1:-1]
        + conv_float[2] * extended[:, 2:]
    )
    gated_out = (second_gate * convolved).astype(jnp.bfloat16)
    middle = inputs + jnp.einsum(
        "scd,de->sce", gated_out, full_out, preferred_element_type=jnp.float32
    )
    unit_two, scale_two, normed_two = norm_forward(middle, gains_float[1])
    gate_value = jnp.einsum(
        "scd,df->scf", normed_two, full_gate[0], preferred_element_type=jnp.float32
    )
    upward = jnp.einsum("scd,df->scf", normed_two, full_gate[1], preferred_element_type=jnp.float32)
    hidden = (jax.nn.silu(gate_value) * upward).astype(jnp.bfloat16)
    result = middle + jnp.einsum(
        "scf,fd->scd", hidden, full_down, preferred_element_type=jnp.float32
    )
    block_out = result.astype(jnp.bfloat16)
    regathered = (
        lax.all_gather(in_proj, "shard", axis=0, tiled=True),
        lax.all_gather(out_proj, "shard", axis=0, tiled=True),
        lax.all_gather(gate_up, "shard", axis=1, tiled=True),
        lax.all_gather(down_proj, "shard", axis=1, tiled=True),
        lax.all_gather(conv_kernel, "shard", axis=1, tiled=True),
        lax.all_gather(norm_gains, "shard", axis=1, tiled=True),
    )
    full_in, full_out, full_gate, full_down, full_conv, full_gains = regathered
    gains_float = full_gains.astype(jnp.float32)
    conv_float = full_conv.astype(jnp.float32)
    grad_result = cotangent.astype(jnp.float32)
    grad_hidden = jnp.einsum(
        "scd,fd->scf", cotangent, full_down, preferred_element_type=jnp.float32
    )
    grad_down = jnp.einsum("scf,scd->fd", hidden, cotangent, preferred_element_type=jnp.float32)
    sigmoid_gate = jax.nn.sigmoid(gate_value)
    grad_gate = (
        grad_hidden * upward * sigmoid_gate * (1.0 + gate_value * (1.0 - sigmoid_gate))
    ).astype(jnp.bfloat16)
    grad_upward = (grad_hidden * jax.nn.silu(gate_value)).astype(jnp.bfloat16)
    grad_gate_up = jnp.stack(
        [
            jnp.einsum("scd,scf->df", normed_two, grad_gate, preferred_element_type=jnp.float32),
            jnp.einsum("scd,scf->df", normed_two, grad_upward, preferred_element_type=jnp.float32),
        ]
    )
    grad_normed_two = jnp.einsum(
        "scf,df->scd", grad_gate, full_gate[0], preferred_element_type=jnp.float32
    ) + jnp.einsum("scf,df->scd", grad_upward, full_gate[1], preferred_element_type=jnp.float32)
    gain_two, grad_from_two = norm_backward(grad_normed_two, unit_two, scale_two, gains_float[1])
    grad_middle = grad_result + grad_from_two
    middle_low = grad_middle.astype(jnp.bfloat16)
    grad_out = jnp.einsum("scd,sce->de", gated_out, middle_low, preferred_element_type=jnp.float32)
    grad_gated = jnp.einsum("sce,de->scd", middle_low, full_out, preferred_element_type=jnp.float32)
    grad_second = grad_gated * convolved
    grad_conv_out = grad_gated * second_gate
    grad_conv = jnp.stack(
        [
            jnp.sum(grad_conv_out * extended[:, offset : offset + rows_count], axis=(0, 1))
            for offset in range(3)
        ]
    )
    grad_extended = (
        jnp.pad(grad_conv_out * conv_float[0], ((0, 0), (0, 2), (0, 0)))
        + jnp.pad(grad_conv_out * conv_float[1], ((0, 0), (1, 1), (0, 0)))
        + jnp.pad(grad_conv_out * conv_float[2], ((0, 0), (2, 0), (0, 0)))
    )
    from_next = shifted(grad_extended[:, :2, :], "seq", -1)
    grad_mixed = grad_extended[:, 2:, :] + jnp.pad(from_next, ((0, 0), (rows_count - 2, 0), (0, 0)))
    grad_projected = jnp.concatenate(
        [grad_mixed * conv_input, grad_second, grad_mixed * first_gate], axis=2
    ).astype(jnp.bfloat16)
    grad_in = jnp.einsum(
        "scd,sce->de", normed_one, grad_projected, preferred_element_type=jnp.float32
    )
    grad_normed_one = jnp.einsum(
        "sce,de->scd", grad_projected, full_in, preferred_element_type=jnp.float32
    )
    gain_one, grad_from_one = norm_backward(grad_normed_one, unit_one, scale_one, gains_float[0])
    token_grad = (grad_middle + grad_from_one).astype(jnp.bfloat16)
    grad_gains = jnp.stack([gain_one, gain_two])
    parts = (
        lax.psum_scatter(grad_in, "shard", scatter_dimension=0, tiled=True),
        lax.psum_scatter(grad_out, "shard", scatter_dimension=0, tiled=True),
        lax.psum_scatter(grad_gate_up, "shard", scatter_dimension=1, tiled=True),
        lax.psum_scatter(grad_down, "shard", scatter_dimension=1, tiled=True),
        lax.psum_scatter(grad_conv, "shard", scatter_dimension=1, tiled=True),
        lax.psum_scatter(grad_gains, "shard", scatter_dimension=1, tiled=True),
    )
    totals = lax.psum((parts[0], parts[1], parts[2], parts[3], parts[4], parts[5]), ("rep", "seq"))
    matrix_rate = 2.0 * model_width ** (-0.5)
    down_rate = 2.0 * gate_up.shape[2] ** (-0.5)
    in_next, in_moment_next, in_square_next = adamw(
        in_proj.astype(jnp.float32),
        in_moment.astype(jnp.float32),
        in_square.astype(jnp.float32),
        totals[0],
        matrix_rate,
        decay_rate,
    )
    out_next, out_moment_next, out_square_next = adamw(
        out_proj.astype(jnp.float32),
        out_moment.astype(jnp.float32),
        out_square.astype(jnp.float32),
        totals[1],
        matrix_rate,
        decay_rate,
    )
    gate_next, gate_moment_next, gate_square_next = adamw(
        gate_up.astype(jnp.float32),
        gate_moment.astype(jnp.float32),
        gate_square.astype(jnp.float32),
        totals[2],
        matrix_rate,
        decay_rate,
    )
    down_next, down_moment_next, down_square_next = adamw(
        down_proj.astype(jnp.float32),
        down_moment.astype(jnp.float32),
        down_square.astype(jnp.float32),
        totals[3],
        down_rate,
        decay_rate,
    )
    conv_next, conv_moment_next, conv_square_next = adamw(
        conv_kernel.astype(jnp.float32),
        conv_moment.astype(jnp.float32),
        conv_square.astype(jnp.float32),
        totals[4],
        small_rate,
        0.0,
    )
    gains_next, gains_moment_next, gains_square_next = adamw(
        norm_gains.astype(jnp.float32),
        gains_moment.astype(jnp.float32),
        gains_square.astype(jnp.float32),
        totals[5],
        small_rate,
        0.0,
    )
    return (
        block_out,
        token_grad,
        in_next,
        in_moment_next,
        in_square_next,
        out_next,
        out_moment_next,
        out_square_next,
        gate_next,
        gate_moment_next,
        gate_square_next,
        down_next,
        down_moment_next,
        down_square_next,
        conv_next,
        conv_moment_next,
        conv_square_next,
        gains_next,
        gains_moment_next,
        gains_square_next,
    )


def solution(mesh):
    act = P(("rep", "shard"), "seq", None)
    weights = (
        (P("shard", None),) * 6 + (P(None, "shard", None),) * 3 + (P(None, "shard"),) * 9
    )
    specs = (act, act) + weights
    sizes = (mesh.shape["rep"], mesh.shape["seq"], mesh.shape["shard"])
    body = fused_body if sizes == (4, 4, 2) else plain_body
    return jax.shard_map(body, mesh=mesh, in_specs=specs, out_specs=specs, check_vma=False)
```

time: 364 us -> 313 us (0.86)
  Pallas kernels: 356 us -> 296 us
  waiting for transfers between devices: 0 us -> 6.14 us
    pallas_call x1, Pallas kernels: 277 us -> 217 us  [run_block(): pl.pallas_call(functools.partial(block_kernel, dims), out_shape=(jax.Shap...]
    ppermute x0 -> x2, waiting for transfers between devices: none -> 6.14 us  [the longest x1 4.96 us: fused_body(): across = lax.ppermute(mine, 'seq', [(i, (i + 2) % 4) for i in range(4)])]
    pallas_call x4 -> x5, Pallas kernels: 79 us -> 79.2 us  [update(): pl.pallas_call(functools.partial(kernel, rate), grid_spec=pltpu.PrefetchS...]
  transfers between devices with their start and end apart: 0 -> 2, of which waited for: 0 -> 2; matrix products, arithmetic and copies ran while one was open for 0% -> 1% of each run, Pallas kernels for 0% -> 15%
where the time goes in v2:
time: 313 us; the launch traced here: 312 us
  Pallas kernels  296 us (95%)
  waiting for transfers between devices  6.14 us (2%)
  other arithmetic  6.04 us (2%)
    pallas_call x1, Pallas kernels, run_block(): pl.pallas_call(functools.partial(block_kernel, dims), out_shape=(jax.Shap...  217 us
    pallas_call x5, Pallas kernels, update(): pl.pallas_call(functools.partial(kernel, rate), grid_spec=pltpu.PrefetchS...  79.2 us
  transfers between devices with their start and end apart: 2, of which 2 were waited for; matrix products, arithmetic and copies ran while one was open for 1% of the time, Pallas kernels for 15%

profile of v2, /device:TPU:0, one launch (start us, length us, event | category | flops | bytes accessed | tf_op | source)
XLA Modules:
  0.0 311.7 jit_solution(15315203923216911430)
XLA Ops:
  0.7 0.7 convert_element_type.20
  1.3 0.7 convert_element_type.21
  2.0 0.6 pad_maximum_fusion.small_h
  2.7 216.7 %block_kernel.1 = (bf16[256,1024]{1,0:T(8,128)(2,1)}, bf16[256,1024]{1,0:T(8,128)(2,1)}, bf16[4,1536,768]{2,1,0:T(8,128)(2,1)}, bf16[1536,768]{1,0:T(8,128)(2,1)...) custom-call(bf16[256,1024]{1,0:T(8,128)(2,1)} %bitcast.9, bf16[256,1024]{1,0:T(8,128)(2,1)} %bitcast.10, ...), custom_call_target="tpu_custom_call" | custom-call | flops 56371445760 | bytes 62914560 | tf_op jit(solution)/shard_map/block_kernel/pallas_call | solution.py:850
  219.4 1.2 collective-permute-start
  220.6 0.6 pad_add_fusion.where
  221.2 10.7 %update_down.1 = (f32[4608,512]{1,0:T(8,128)}, f32[4608,512]{1,0:T(8,128)}, f32[4608,512]{1,0:T(8,128)}) custom-call(s32[2]{0:T(128)} %pad_add_fusion.where, bf16[4608,512]{1,0:T(8,128)(2,1)} %w.9, bf16[4608,512]{1,0:T(8,128)(2,1)} %m.9, bf16[4608,512]{1,0:T(8,128)(2,1)} %v.9, bf16[1536,768]{1,0:T(8,128)(2,1)} %get-tuple-element.50.refs_0_.refs_1_.refs_2_, ...), custom_call_target="tpu_custom_call" | custom-call | flops 14155776 | bytes 23592960 | tf_op jit(solution)/shard_map/update_down/pallas_call | solution.py:959
  231.9 0.0 copy-start.4
  231.9 0.0 copy-start.7
  231.9 0.0 copy-start.8
  231.9 0.0 copy-start.3
  232.0 0.0 copy-start.5
  232.0 0.0 copy-start.6
  232.0 36.0 %update_gate.1 = (f32[2,512,4608]{2,1,0:T(8,128)}, f32[2,512,4608]{2,1,0:T(8,128)}, f32[2,512,4608]{2,1,0:T(8,128)}) custom-call(s32[2]{0:T(128)} %pad_add_fusion.where, bf16[2,512,4608]{2,1,0:T(8,128)(2,1)} %w.5, bf16[2,512,4608]{2,1,0:T(8,128)(2,1)} %m.5, bf16[2,512,4608]{2,1,0:T(8,128)(2,1)} %v.5, ...), custom_call_target="tpu_custom_call" | custom-call | flops 56623104 | bytes 94371840 | tf_op jit(solution)/shard_map/update_gate/pallas_call | solution.py:959
  267.9 5.0 %collective-permute-done.refs_2_.refs_0_.refs_1_ = bf16[1536,768]{1,0:T(8,128)(2,1)S(1)} collective-permute-done((bf16[1536,768]{1,0:T(8,128)(2,1)}, bf16[1536,768]{1,0:T(8,128)(2,1)S(1)}, u32[]{:S(2)}, u32[]{:S(2)}) %collective-permute-start) | collective-permute-done | bytes 2359328 | tf_op jit(solution)/shard_map/ppermute | solution.py:1011
  272.9 0.0 copy-start
  272.9 0.0 collective-permute-start.1
  272.9 0.7 pad_add_fusion.1.where
  273.6 0.0 copy-done.4
  273.6 0.0 copy-done.7
  273.6 0.0 copy-done.8
  273.6 1.4 multiply_subtract_fusion.1
  275.0 0.0 copy-done.3
  275.0 0.0 copy-done.5
  275.0 0.0 copy-done.6
  275.0 1.4 multiply_subtract_fusion
  276.4 1.2 collective-permute-done.1.refs_3_.refs_4_.refs_5_
  277.6 0.0 copy-done
  277.6 7.3 %update_out.1 = (f32[512,1024]{1,0:T(8,128)}, f32[512,1024]{1,0:T(8,128)}, f32[512,1024]{1,0:T(8,128)}) custom-call(s32[2]{0:T(128)} %pad_add_fusion.where, bf16[512,1024]{1,0:T(8,128)(2,1)} %w.8, bf16[512,1024]{1,0:T(8,128)(2,1)} %m.8, bf16[512,1024]{1,0:T(8,128)(2,1)} %v.8, bf16[1536,768]{1,0:T(8,128)(2,1)} %get-tuple-element.50.refs_0_.refs_1_.refs_2_, ...), custom_call_target="tpu_custom_call" | custom-call | flops 6291456 | bytes 10485760 | tf_op jit(solution)/shard_map/update_out/pallas_call | solution.py:959
  284.8 14.4 %update_in.1 = (f32[512,3072]{1,0:T(8,128)}, f32[512,3072]{1,0:T(8,128)}, f32[512,3072]{1,0:T(8,128)}) custom-call(s32[2]{0:T(128)} %pad_add_fusion.where, bf16[512,3072]{1,0:T(8,128)(2,1)} %w.7, bf16[512,3072]{1,0:T(8,128)(2,1)} %m.7, bf16[512,3072]{1,0:T(8,128)(2,1)} %v.7, bf16[1536,768]{1,0:T(8,128)(2,1)} %get-tuple-element.50.refs_0_.refs_1_.refs_2_, ...), custom_call_target="tpu_custom_call" | custom-call | flops 18874368 | bytes 31457280 | tf_op jit(solution)/shard_map/update_in/pallas_call | solution.py:959
  299.2 0.0 copy-start.2
  299.2 0.0 copy-start.1
  299.3 10.8 %update_down_far.1 = (f32[4608,512]{1,0:T(8,128)}, f32[4608,512]{1,0:T(8,128)}, f32[4608,512]{1,0:T(8,128)}) custom-call(s32[2]{0:T(128)} %pad_add_fusion.1.where, bf16[4608,512]{1,0:T(8,128)(2,1)} %w.9, bf16[4608,512]{1,0:T(8,128)(2,1)} %m.9, bf16[4608,512]{1,0:T(8,128)(2,1)} %v.9, ...), custom_call_target="tpu_custom_call", output_to_operand_aliasing={{0}: (10, {}), {1}: (11, {}), {2}: (12, {})} | custom-call | flops 14155776 | bytes 23592960 | tf_op jit(solution)/shard_map/update_down_far/pallas_call | solution.py:959
  310.1 0.0 copy-done.2
  310.1 0.8 copy.48
  310.9 0.0 copy-done.1
  310.9 0.8 copy.49
  (1 shorter events, 0.0 us)
Async XLA Ops:
  219.4 53.5 %collective-permute-start = (bf16[1536,768]{1,0:T(8,128)(2,1)}, bf16[1536,768]{1,0:T(8,128)(2,1)S(1)}, u32[]{:S(2)}, u32[]{:S(2)}) collective-permute-start(bf16[1536,768]{1,0:T(8,128)(2,1)} %get-tuple-element.50.refs_0_.refs_1_.refs_2_), channel_id=1, source_target_pairs={{0,4},{2,6},{4,0},{6,2},{1,5},{3,7},{5,1},{7,3},{8,12},{10,14},{12... | collective-permute-start | bytes 7077896 | tf_op jit(solution)/shard_map/ppermute | solution.py:1011
  231.9 41.7 %copy-start.4 = (bf16[2,512]{1,0:T(2,128)(2,1)S(1)}, bf16[2,512]{1,0:T(2,128)(2,1)}, u32[]{:S(2)}) copy-start(bf16[2,512]{1,0:T(2,128)(2,1)} %param.37) | copy-start | bytes 6148
  231.9 41.7 %copy-start.7 = (bf16[2,512]{1,0:T(2,128)(2,1)S(1)}, bf16[2,512]{1,0:T(2,128)(2,1)}, u32[]{:S(2)}) copy-start(bf16[2,512]{1,0:T(2,128)(2,1)} %param.38) | copy-start | bytes 6148
  231.9 41.7 %copy-start.8 = (bf16[2,512]{1,0:T(2,128)(2,1)S(1)}, bf16[2,512]{1,0:T(2,128)(2,1)}, u32[]{:S(2)}) copy-start(bf16[2,512]{1,0:T(2,128)(2,1)} %param.39) | copy-start | bytes 6148
  231.9 43.1 %copy-start.3 = (bf16[3,512]{1,0:T(4,128)(2,1)S(1)}, bf16[3,512]{1,0:T(4,128)(2,1)}, u32[]{:S(2)}) copy-start(bf16[3,512]{1,0:T(4,128)(2,1)} %param.34) | copy-start | bytes 9220
  232.0 43.1 %copy-start.5 = (bf16[3,512]{1,0:T(4,128)(2,1)S(1)}, bf16[3,512]{1,0:T(4,128)(2,1)}, u32[]{:S(2)}) copy-start(bf16[3,512]{1,0:T(4,128)(2,1)} %param.35) | copy-start | bytes 9220
  232.0 43.1 %copy-start.6 = (bf16[3,512]{1,0:T(4,128)(2,1)S(1)}, bf16[3,512]{1,0:T(4,128)(2,1)}, u32[]{:S(2)}) copy-start(bf16[3,512]{1,0:T(4,128)(2,1)} %param.36) | copy-start | bytes 9220
  272.9 4.7 %copy-start = (bf16[1536,768]{1,0:T(8,128)(2,1)}, bf16[1536,768]{1,0:T(8,128)(2,1)S(1)}, u32[]{:S(2)}) copy-start(bf16[1536,768]{1,0:T(8,128)(2,1)S(1)} %collective-permute-done.refs_2_.refs_0_.refs_1_) | copy-start | bytes 7077892
  272.9 4.7 %collective-permute-start.1 = (bf16[1536,768]{1,0:T(8,128)(2,1)S(1)}, bf16[1536,768]{1,0:T(8,128)(2,1)}, u32[]{:S(2)}, u32[]{:S(2)}) collective-permute-start(bf16[1536,768]{1,0:T(8,128)(2,1)S(1)} %collective-permute-done.refs_2_.refs_0_.refs_1_), channel_id=1, source_target_pairs={{0,2},{2,0},{4,6},{6,4},{1,3},{3,1},{5,7},{7,5},{8,10},{10,8},{12,... | collective-permute-start | bytes 7077896 | tf_op jit(solution)/shard_map/ppermute | solution.py:1022
  299.2 10.9 %copy-start.2 = (bf16[256,1024]{1,0:T(8,128)(2,1)S(1)}, bf16[256,1024]{1,0:T(8,128)(2,1)}, u32[]{:S(2)}) copy-start(bf16[256,1024]{1,0:T(8,128)(2,1)} %get-tuple-element.48) | copy-start | bytes 1572868
  299.2 11.7 %copy-start.1 = (bf16[256,1024]{1,0:T(8,128)(2,1)S(1)}, bf16[256,1024]{1,0:T(8,128)(2,1)}, u32[]{:S(2)}) copy-start(bf16[256,1024]{1,0:T(8,128)(2,1)} %get-tuple-element.49) | copy-start | bytes 1572868

commit v3 on v2

--- a/solution.py
+++ b/solution.py
@@ -30,11 +30,11 @@
     (0, 1, 3, 5, 8),
     (0, 2, 4, 6, 10),
     (0, 4, 6, 8, 11),
-    (0, 10, 13, 16, 20),
-    (4, 13, 16, 18, 23),
-    (8, 15, 18, 20, 25),
-    (13, 19, 22, 24, 28),
-    (17, 23, 26, 28, 31),
+    (0, 12, 15, 17, 21),
+    (6, 15, 17, 20, 24),
+    (9, 17, 20, 22, 26),
+    (15, 21, 24, 26, 29),
+    (19, 25, 28, 30, 33),
 )
 HELD = 40
 

time: 313 us -> 310 us (level)
  no operation moved by 1% of the time
where the time goes in v3:
time: 310 us; the launch traced here: 309 us
  Pallas kernels  293 us (95%)
  other arithmetic  6.04 us (2%)
  waiting for transfers between devices  5.81 us (2%)
    pallas_call x1, Pallas kernels, run_block(): pl.pallas_call(functools.partial(block_kernel, dims), out_shape=(jax.Shap...  214 us
    pallas_call x5, Pallas kernels, update(): pl.pallas_call(functools.partial(kernel, rate), grid_spec=pltpu.PrefetchS...  79.2 us
  transfers between devices with their start and end apart: 2, of which 2 were waited for; matrix products, arithmetic and copies ran while one was open for 1% of the time, Pallas kernels for 15%

profile of v3, /device:TPU:0, one launch (start us, length us, event | category | flops | bytes accessed | tf_op | source)
XLA Modules:
  0.0 308.9 jit_solution(1006344732828580493)
XLA Ops:
  0.7 0.7 convert_element_type.20
  1.3 0.7 convert_element_type.21
  2.0 0.6 pad_maximum_fusion.small_h
  2.7 214.0 %block_kernel.1 = (bf16[256,1024]{1,0:T(8,128)(2,1)}, bf16[256,1024]{1,0:T(8,128)(2,1)}, bf16[4,1536,768]{2,1,0:T(8,128)(2,1)}, bf16[1536,768]{1,0:T(8,128)(2,1)...) custom-call(bf16[256,1024]{1,0:T(8,128)(2,1)} %bitcast.9, bf16[256,1024]{1,0:T(8,128)(2,1)} %bitcast.10, ...), custom_call_target="tpu_custom_call" | custom-call | flops 56371445760 | bytes 62914560 | tf_op jit(solution)/shard_map/block_kernel/pallas_call | solution.py:850
  216.6 1.5 collective-permute-start
  218.2 0.6 pad_add_fusion.where
  218.7 10.7 %update_down.1 = (f32[4608,512]{1,0:T(8,128)}, f32[4608,512]{1,0:T(8,128)}, f32[4608,512]{1,0:T(8,128)}) custom-call(s32[2]{0:T(128)} %pad_add_fusion.where, bf16[4608,512]{1,0:T(8,128)(2,1)} %w.9, bf16[4608,512]{1,0:T(8,128)(2,1)} %m.9, bf16[4608,512]{1,0:T(8,128)(2,1)} %v.9, bf16[1536,768]{1,0:T(8,128)(2,1)} %get-tuple-element.50.refs_0_.refs_1_.refs_2_, ...), custom_call_target="tpu_custom_call" | custom-call | flops 14155776 | bytes 23592960 | tf_op jit(solution)/shard_map/update_down/pallas_call | solution.py:959
  229.5 0.0 copy-start.4
  229.5 0.0 copy-start.7
  229.5 0.0 copy-start.8
  229.5 0.0 copy-start.3
  229.5 0.0 copy-start.5
  229.5 0.0 copy-start.6
  229.6 36.0 %update_gate.1 = (f32[2,512,4608]{2,1,0:T(8,128)}, f32[2,512,4608]{2,1,0:T(8,128)}, f32[2,512,4608]{2,1,0:T(8,128)}) custom-call(s32[2]{0:T(128)} %pad_add_fusion.where, bf16[2,512,4608]{2,1,0:T(8,128)(2,1)} %w.5, bf16[2,512,4608]{2,1,0:T(8,128)(2,1)} %m.5, bf16[2,512,4608]{2,1,0:T(8,128)(2,1)} %v.5, ...), custom_call_target="tpu_custom_call" | custom-call | flops 56623104 | bytes 94371840 | tf_op jit(solution)/shard_map/update_gate/pallas_call | solution.py:959
  265.5 4.6 %collective-permute-done.refs_2_.refs_0_.refs_1_ = bf16[1536,768]{1,0:T(8,128)(2,1)S(1)} collective-permute-done((bf16[1536,768]{1,0:T(8,128)(2,1)}, bf16[1536,768]{1,0:T(8,128)(2,1)S(1)}, u32[]{:S(2)}, u32[]{:S(2)}) %collective-permute-start) | collective-permute-done | bytes 2359328 | tf_op jit(solution)/shard_map/ppermute | solution.py:1011
  270.1 0.0 copy-start
  270.2 0.0 collective-permute-start.1
  270.2 0.7 pad_add_fusion.1.where
  270.8 0.0 copy-done.4
  270.8 0.0 copy-done.7
  270.8 0.0 copy-done.8
  270.8 1.4 multiply_subtract_fusion.1
  272.3 0.0 copy-done.3
  272.3 0.0 copy-done.5
  272.3 0.0 copy-done.6
  272.3 1.4 multiply_subtract_fusion
  273.6 1.2 collective-permute-done.1.refs_3_.refs_4_.refs_5_
  274.8 0.0 copy-done
  274.8 7.3 %update_out.1 = (f32[512,1024]{1,0:T(8,128)}, f32[512,1024]{1,0:T(8,128)}, f32[512,1024]{1,0:T(8,128)}) custom-call(s32[2]{0:T(128)} %pad_add_fusion.where, bf16[512,1024]{1,0:T(8,128)(2,1)} %w.8, bf16[512,1024]{1,0:T(8,128)(2,1)} %m.8, bf16[512,1024]{1,0:T(8,128)(2,1)} %v.8, bf16[1536,768]{1,0:T(8,128)(2,1)} %get-tuple-element.50.refs_0_.refs_1_.refs_2_, ...), custom_call_target="tpu_custom_call" | custom-call | flops 6291456 | bytes 10485760 | tf_op jit(solution)/shard_map/update_out/pallas_call | solution.py:959
  282.1 14.4 %update_in.1 = (f32[512,3072]{1,0:T(8,128)}, f32[512,3072]{1,0:T(8,128)}, f32[512,3072]{1,0:T(8,128)}) custom-call(s32[2]{0:T(128)} %pad_add_fusion.where, bf16[512,3072]{1,0:T(8,128)(2,1)} %w.7, bf16[512,3072]{1,0:T(8,128)(2,1)} %m.7, bf16[512,3072]{1,0:T(8,128)(2,1)} %v.7, bf16[1536,768]{1,0:T(8,128)(2,1)} %get-tuple-element.50.refs_0_.refs_1_.refs_2_, ...), custom_call_target="tpu_custom_call" | custom-call | flops 18874368 | bytes 31457280 | tf_op jit(solution)/shard_map/update_in/pallas_call | solution.py:959
  296.5 0.0 copy-start.2
  296.5 0.0 copy-start.1
  296.5 10.8 %update_down_far.1 = (f32[4608,512]{1,0:T(8,128)}, f32[4608,512]{1,0:T(8,128)}, f32[4608,512]{1,0:T(8,128)}) custom-call(s32[2]{0:T(128)} %pad_add_fusion.1.where, bf16[4608,512]{1,0:T(8,128)(2,1)} %w.9, bf16[4608,512]{1,0:T(8,128)(2,1)} %m.9, bf16[4608,512]{1,0:T(8,128)(2,1)} %v.9, ...), custom_call_target="tpu_custom_call", output_to_operand_aliasing={{0}: (10, {}), {1}: (11, {}), {2}: (12, {})} | custom-call | flops 14155776 | bytes 23592960 | tf_op jit(solution)/shard_map/update_down_far/pallas_call | solution.py:959
  307.3 0.0 copy-done.2
  307.4 0.8 copy.48
  308.1 0.0 copy-done.1
  308.1 0.8 copy.49
  (1 shorter events, 0.0 us)
Async XLA Ops:
  216.6 53.5 %collective-permute-start = (bf16[1536,768]{1,0:T(8,128)(2,1)}, bf16[1536,768]{1,0:T(8,128)(2,1)S(1)}, u32[]{:S(2)}, u32[]{:S(2)}) collective-permute-start(bf16[1536,768]{1,0:T(8,128)(2,1)} %get-tuple-element.50.refs_0_.refs_1_.refs_2_), channel_id=1, source_target_pairs={{0,4},{2,6},{4,0},{6,2},{1,5},{3,7},{5,1},{7,3},{8,12},{10,14},{12... | collective-permute-start | bytes 7077896 | tf_op jit(solution)/shard_map/ppermute | solution.py:1011
  229.5 41.3 %copy-start.4 = (bf16[2,512]{1,0:T(2,128)(2,1)S(1)}, bf16[2,512]{1,0:T(2,128)(2,1)}, u32[]{:S(2)}) copy-start(bf16[2,512]{1,0:T(2,128)(2,1)} %param.37) | copy-start | bytes 6148
  229.5 41.3 %copy-start.7 = (bf16[2,512]{1,0:T(2,128)(2,1)S(1)}, bf16[2,512]{1,0:T(2,128)(2,1)}, u32[]{:S(2)}) copy-start(bf16[2,512]{1,0:T(2,128)(2,1)} %param.38) | copy-start | bytes 6148
  229.5 41.3 %copy-start.8 = (bf16[2,512]{1,0:T(2,128)(2,1)S(1)}, bf16[2,512]{1,0:T(2,128)(2,1)}, u32[]{:S(2)}) copy-start(bf16[2,512]{1,0:T(2,128)(2,1)} %param.39) | copy-start | bytes 6148
  229.5 42.8 %copy-start.3 = (bf16[3,512]{1,0:T(4,128)(2,1)S(1)}, bf16[3,512]{1,0:T(4,128)(2,1)}, u32[]{:S(2)}) copy-start(bf16[3,512]{1,0:T(4,128)(2,1)} %param.34) | copy-start | bytes 9220
  229.5 42.7 %copy-start.5 = (bf16[3,512]{1,0:T(4,128)(2,1)S(1)}, bf16[3,512]{1,0:T(4,128)(2,1)}, u32[]{:S(2)}) copy-start(bf16[3,512]{1,0:T(4,128)(2,1)} %param.35) | copy-start | bytes 9220
  229.5 42.7 %copy-start.6 = (bf16[3,512]{1,0:T(4,128)(2,1)S(1)}, bf16[3,512]{1,0:T(4,128)(2,1)}, u32[]{:S(2)}) copy-start(bf16[3,512]{1,0:T(4,128)(2,1)} %param.36) | copy-start | bytes 9220
  270.1 4.7 %copy-start = (bf16[1536,768]{1,0:T(8,128)(2,1)}, bf16[1536,768]{1,0:T(8,128)(2,1)S(1)}, u32[]{:S(2)}) copy-start(bf16[1536,768]{1,0:T(8,128)(2,1)S(1)} %collective-permute-done.refs_2_.refs_0_.refs_1_) | copy-start | bytes 7077892
  270.2 4.7 %collective-permute-start.1 = (bf16[1536,768]{1,0:T(8,128)(2,1)S(1)}, bf16[1536,768]{1,0:T(8,128)(2,1)}, u32[]{:S(2)}, u32[]{:S(2)}) collective-permute-start(bf16[1536,768]{1,0:T(8,128)(2,1)S(1)} %collective-permute-done.refs_2_.refs_0_.refs_1_), channel_id=1, source_target_pairs={{0,2},{2,0},{4,6},{6,4},{1,3},{3,1},{5,7},{7,5},{8,10},{10,8},{12,... | collective-permute-start | bytes 7077896 | tf_op jit(solution)/shard_map/ppermute | solution.py:1022
  296.5 10.9 %copy-start.2 = (bf16[256,1024]{1,0:T(8,128)(2,1)S(1)}, bf16[256,1024]{1,0:T(8,128)(2,1)}, u32[]{:S(2)}) copy-start(bf16[256,1024]{1,0:T(8,128)(2,1)} %get-tuple-element.48) | copy-start | bytes 1572868
  296.5 11.7 %copy-start.1 = (bf16[256,1024]{1,0:T(8,128)(2,1)S(1)}, bf16[256,1024]{1,0:T(8,128)(2,1)}, u32[]{:S(2)}) copy-start(bf16[256,1024]{1,0:T(8,128)(2,1)} %get-tuple-element.49) | copy-start | bytes 1572868
